TPU v7x, 32 devices: a whole 2x2x4 slice. The times are simulated.
32 devices in a mesh: mode: 8 (over z, x), slab: 4 (over y, core).
Axes of the slice: x: 2, y: 2, z: 4, core: 2. Of those that a mesh axis runs over, the one named last changes fastest.
Arguments:
- field: float32 [128, 16, 64, 128], P('mode', 'slab'), may hold values from -6 to 6
- coefficient_fields: float32 [16, 16, 64, 128], P(None, 'slab', 'mode'), may hold values from -6 to 6
- triple_blocks: float32 [16, 4, 32, 64], replicated, may hold values from -0.1875 to 0.1875
- block_pattern: int32 [16, 4, 2], replicated, may hold values from 0 to 3
Outputs:
- result: float32 [128, 16, 64, 128], P('mode', 'slab')
All inputs are finite; a program needn't handle non-finite values.
Results may differ from a plain program's by a relative error of at most 0.0003.
Values sent between devices are 32-bit elements; how exact they have to be, the bound alone decides.
No kernel may reach another device: no remote copies, remote signals or barrier semaphores. Data moves between devices by JAX's collectives and lax.ppermute only.
A program may use at most 128 MiB of HBM per device.

v0:
```python
import jax
import jax.numpy as jnp
from jax import lax
from jax.sharding import PartitionSpec as P


def from_behind(value, axis, steps):
    count = lax.axis_size(axis)
    first, last = (max(0, -steps), min(count, count - steps))
    return lax.ppermute(value, axis, [(source, source + steps) for source in range(first, last)])


def dense_matrices(triple_blocks, block_pattern):
    fields = triple_blocks.shape[0]
    row_blocks = triple_blocks.shape[1]
    block_size = triple_blocks.shape[2]
    stored = block_pattern.shape[2]
    pieces = triple_blocks.reshape(fields, row_blocks, block_size, stored, block_size)
    targets = jnp.arange(row_blocks, dtype=jnp.int32)
    selector = (block_pattern[..., None] == targets).astype(jnp.float32)
    dense = jnp.einsum("krisj,krsc->kricj", pieces, selector, precision=lax.Precision.HIGHEST)
    return dense.reshape(fields, row_blocks * block_size, row_blocks * block_size)


def couple_planes(gradient, weights_local, matrices):
    depth_count = gradient.shape[2]
    fields = matrices.shape[0]

    def plane_step(depth, output):
        plane = lax.dynamic_index_in_dim(gradient, depth, 2, keepdims=False)
        shape = plane.shape
        flat = plane.reshape(3, shape[1], -1)
        weights_here = lax.dynamic_index_in_dim(weights_local, depth, 1, keepdims=False).reshape(
            fields, -1
        )
        products = jnp.einsum("kij,djn->kdin", matrices, flat, precision=lax.Precision.HIGHEST)
        total = jnp.einsum("kdin,kn->din", products, weights_here, precision=lax.Precision.HIGHEST)
        return lax.dynamic_update_slice_in_dim(output, total.reshape(shape)[:, :, None], depth, 2)

    return lax.fori_loop(0, depth_count, plane_step, jnp.zeros_like(gradient))


def lower_part(flux_z):
    previous = from_behind(flux_z[:, -1:], "slab", 1)
    shifted = jnp.concatenate([previous, flux_z[:, :-1]], axis=1)
    return shifted - flux_z


def backward_part(flux, axis_number):
    size = flux.shape[axis_number]
    first = lax.slice_in_dim(flux, 0, 1, axis=axis_number)
    rest = lax.slice_in_dim(flux, 0, size - 1, axis=axis_number)
    return jnp.concatenate([jnp.zeros_like(first), rest], axis=axis_number) - flux


def body(field, coefficient_fields, triple_blocks, block_pattern):
    matrices = dense_matrices(triple_blocks, block_pattern)
    upper_plane = from_behind(field[:, :1], "slab", -1)
    extended = jnp.concatenate([field, upper_plane], axis=1)
    centre = extended[:, :-1]
    grad_x = jnp.concatenate([centre[..., 1:], jnp.zeros_like(centre[..., :1])], axis=-1) - centre
    grad_y = jnp.concatenate([centre[:, :, 1:], jnp.zeros_like(centre[:, :, :1])], axis=2) - centre
    grad_z = extended[:, 1:] - centre
    gradient = jnp.stack([grad_x, grad_y, grad_z])
    regrouped = lax.all_to_all(gradient, "mode", split_axis=3, concat_axis=1, tiled=True)
    flux = couple_planes(regrouped, coefficient_fields, matrices)
    returned = lax.all_to_all(flux, "mode", split_axis=1, concat_axis=3, tiled=True)
    flux_x, flux_y, flux_z = (returned[0], returned[1], returned[2])
    part_x = backward_part(flux_x, 3)
    part_y = backward_part(flux_y, 2)
    result = part_x + part_y + lower_part(flux_z)
    return result


def solution(mesh):
    in_specs = (P("mode", "slab", None, None), P(None, "slab", "mode", None), P(), P())
    out_specs = P("mode", "slab", None, None)
    return jax.shard_map(body, mesh=mesh, in_specs=in_specs, out_specs=out_specs, check_vma=False)
```

profile of v0, /device:TPU:1, one launch (start us, length us, event | category | flops | bytes accessed | tf_op | source)
XLA Modules:
  0.0 703.1 jit_solution(13221493063612826348)
XLA Ops:
  1.6 2.0 collective-permute-start
  3.6 2.9 copy.8
  9.3 2.1 subtract_bitcast_fusion.1
  11.4 1.6 collective-permute-done
  14.1 4.4 pad_maximum_fusion
  18.5 5.9 all-to-all-start
  25.7 6.7 convolution_bitcast_fusion.1
  32.4 4.5 reshape.37
  36.9 126.6 %all-to-all-done = f32[3,16,4,64,128]{4,2,1,0,3:T(4,128)} async-done(((f32[3,16,4,64,128]{4,2,1,0,3:T(4,128)}), f32[3,16,4,64,128]{4,2,1,0,3:T(4,128)}, u32[]{:S(2)}, u32[]{:S(2)}) %all-to-all-start) | async-done | bytes 6291488 | tf_op jit(solution)/shard_map/all_to_all | solution.py:65
  163.5 11.0 %copy.15 = f32[3,8,16,4,8,128]{5,4,3,2,1,0:T(8,128)} copy(f32[3,8,16,4,8,128]{5,3,2,0,4,1:T(4,128)} %bitcast.12) | data formatting | bytes 12582912 | tf_op jit(solution)/shard_map/all_to_all | solution.py:65
  174.5 373.8 %while.13 = (s32[]{:T(128)}, f32[3,128,4,8,128]{4,3,2,0,1:T(8,128)}, f32[16,4,8,128]{3,2,1,0:T(8,128)}, f32[3,128,4,8,128]{4,3,2,1,0:T(8,128)}, f32[16,128,128]{2,1,0:T(8,128)}, /*index=5*/s32[]{:T(128)}) while((s32[]{:T(128)}, f32[3,128,4,8,128]{4,3,2,0,1:T(8,128)}, f32[16,4,8,128]{3,2,1,0:T(8,128)}, f32[3,128,4,8,128]{4,3,2,1,0:T(8,128)}, ...), condition=%wide.region_1.2_spmd, body=%wide.region_0.1_spmd.sunk | while | flops 9675866112 | bytes 70713928 | solution.py:40
  174.7 1.5 constant_dynamic-slice_fusion.4
  176.5 24.0 %convolution_bitcast_fusion.3 = f32[1024,16,3,128]{3,0,1,2:T(8,128)} fusion(f32[3,128,1024,1]{2,1,0,3:T(8,128)S(1)} %reshape.45, f32[16,128,128]{2,1,0:T(8,128)} %get-tuple-element.164), kind=kOutput, calls=%fused_computation.2.clone.1 | convolution fusion | flops 9663676416 | bytes 27787264 | tf_op jit(solution)/shard_map/while/body/eval_jaxpr/kij,djn->kdin/dot_general | solution.py:36
  201.6 64.3 %fusion.17 = f32[1024,3,128]{2,0,1:T(8,128)S(1)} fusion(f32[1024,16,3,128]{3,0,1,2:T(8,128)} %convolution_bitcast_fusion.3, f32[1024,16]{1,0:T(8,128)S(1)} %copy.68), kind=kLoop, calls=%fused_computation.1.clone.1 | loop fusion | flops 12189696 | bytes 26804224 | tf_op jit(solution)/shard_map/while
  269.8 24.0 %convolution_bitcast_fusion.3 = f32[1024,16,3,128]{3,0,1,2:T(8,128)} fusion(f32[3,128,1024,1]{2,1,0,3:T(8,128)S(1)} %reshape.45, f32[16,128,128]{2,1,0:T(8,128)} %get-tuple-element.164), kind=kOutput, calls=%fused_computation.2.clone.1 | convolution fusion | flops 9663676416 | bytes 27787264 | tf_op jit(solution)/shard_map/while/body/eval_jaxpr/kij,djn->kdin/dot_general | solution.py:36
  294.8 64.3 %fusion.17 = f32[1024,3,128]{2,0,1:T(8,128)S(1)} fusion(f32[1024,16,3,128]{3,0,1,2:T(8,128)} %convolution_bitcast_fusion.3, f32[1024,16]{1,0:T(8,128)S(1)} %copy.68), kind=kLoop, calls=%fused_computation.1.clone.1 | loop fusion | flops 12189696 | bytes 26804224 | tf_op jit(solution)/shard_map/while
  363.2 24.1 %convolution_bitcast_fusion.3 = f32[1024,16,3,128]{3,0,1,2:T(8,128)} fusion(f32[3,128,1024,1]{2,1,0,3:T(8,128)S(1)} %reshape.45, f32[16,128,128]{2,1,0:T(8,128)} %get-tuple-element.164), kind=kOutput, calls=%fused_computation.2.clone.1 | convolution fusion | flops 9663676416 | bytes 27787264 | tf_op jit(solution)/shard_map/while/body/eval_jaxpr/kij,djn->kdin/dot_general | solution.py:36
  388.3 64.3 %fusion.17 = f32[1024,3,128]{2,0,1:T(8,128)S(1)} fusion(f32[1024,16,3,128]{3,0,1,2:T(8,128)} %convolution_bitcast_fusion.3, f32[1024,16]{1,0:T(8,128)S(1)} %copy.68), kind=kLoop, calls=%fused_computation.1.clone.1 | loop fusion | flops 12189696 | bytes 26804224 | tf_op jit(solution)/shard_map/while
  456.5 24.0 %convolution_bitcast_fusion.3 = f32[1024,16,3,128]{3,0,1,2:T(8,128)} fusion(f32[3,128,1024,1]{2,1,0,3:T(8,128)S(1)} %reshape.45, f32[16,128,128]{2,1,0:T(8,128)} %get-tuple-element.164), kind=kOutput, calls=%fused_computation.2.clone.1 | convolution fusion | flops 9663676416 | bytes 27787264 | tf_op jit(solution)/shard_map/while/body/eval_jaxpr/kij,djn->kdin/dot_general | solution.py:36
  481.6 64.3 %fusion.17 = f32[1024,3,128]{2,0,1:T(8,128)S(1)} fusion(f32[1024,16,3,128]{3,0,1,2:T(8,128)} %convolution_bitcast_fusion.3, f32[1024,16]{1,0:T(8,128)S(1)} %copy.68), kind=kLoop, calls=%fused_computation.1.clone.1 | loop fusion | flops 12189696 | bytes 26804224 | tf_op jit(solution)/shard_map/while
  548.3 141.5 %all_to_all.33 = f32[3,128,4,8,128]{4,3,2,0,1:T(8,128)S(1)} all-to-all(f32[3,128,4,8,128]{4,3,2,0,1:T(8,128)} %get-tuple-element.99), channel_id=1, replica_groups=mesh['mode'=8,'slab'=4] {'mode'}, dimensions={1} | all-to-all | bytes 12582912 | tf_op jit(solution)/shard_map/all_to_all | solution.py:67
  690.9 3.4 collective-permute-start.1
  695.0 5.3 collective-permute-done.1
  700.4 2.3 fusion.5
  (50 shorter events, 26.8 us)
Async XLA Ops:
  1.6 11.4 %collective-permute-start = (f32[16,1,64,128]{3,1,0,2:T(1,128)S(1)}, f32[16,1,64,128]{3,1,0,2:T(1,128)S(1)}, u32[]{:S(2)}, u32[]{:S(2)}) collective-permute-start(f32[16,1,64,128]{3,1,0,2:T(1,128)S(1)} %copy.12), channel_id=1, source_target_pairs={{1,0},{2,1},{3,2},{5,4},{6,5},{7,6},{9,8},{10,9},{11,10},{13,12},{... | collective-permute-start | bytes 1572872 | tf_op jit(solution)/shard_map/ppermute | solution.py:10
  7.7 1.6 copy-start
  18.5 5.9 copy-start.1
  18.5 145.1 %all-to-all-start = ((f32[3,16,4,64,128]{4,2,1,0,3:T(4,128)}), f32[3,16,4,64,128]{4,2,1,0,3:T(4,128)}, u32[]{:S(2)}, u32[]{:S(2)}) async-start(f32[3,16,4,64,128]{4,2,1,0,3:T(4,128)} %pad_maximum_fusion), calls=%async_computation | async-start | bytes 12582912 | tf_op jit(solution)/shard_map/all_to_all | solution.py:65
  24.4 1.2 copy-start.2
  690.9 9.5 %collective-permute-start.1 = (f32[16,1,64,128]{3,2,1,0:T(8,128)S(1)}, f32[16,1,64,128]{3,2,1,0:T(8,128)S(1)}, u32[]{:S(2)}, u32[]{:S(2)}) collective-permute-start(f32[16,1,64,128]{3,2,1,0:T(8,128)S(1)} %slice.54), channel_id=1, source_target_pairs={{0,1},{1,2},{2,3},{4,5},{5,6},{6,7},{8,9},{9,10},{10,11},{12,13},{... | collective-permute-start | bytes 1572872 | tf_op jit(solution)/shard_map/ppermute | solution.py:10
where the time goes:
time: 716 us; the launch traced here: 703 us
  other arithmetic  267 us (37%)
  blocking collectives  141 us (20%)
  waiting for transfers between devices  134 us (19%)
  matrix products  103 us (14%)
  local copies, waits for them, and re-layouts  45.7 us (6%)
  starting transfers between devices  11.2 us (2%)
    while x4, other arithmetic  257 us
    all_to_all x1, blocking collectives, body(): lax.all_to_all(flux, 'mode', split_axis=1, concat_axis=3, tiled=True)  141 us
    all_to_all x1, waiting for transfers between devices, body(): lax.all_to_all(gradient, 'mode', split_axis=3, concat_axis=1, tiled=True)  127 us
    dot_general x4, matrix products, plane_step(): jnp.einsum('kij,djn->kdin', matrices, flat, precision=lax.Precision.HIGHEST)  96.1 us
  transfers between devices with their start and end apart: 3, of which 3 were waited for; matrix products, arithmetic and copies ran while one was open for 3% of the time, Pallas kernels for 0%

commit v1 on v0

v1 whole, which is shorter than its diff:
```python
import functools

import jax
import jax.numpy as jnp
from jax import lax
from jax.experimental import pallas as pl
from jax.experimental.pallas import tpu as pltpu
from jax.sharding import PartitionSpec as P

F32 = jnp.float32
BF16 = jnp.bfloat16
VMEM = pl.BlockSpec(memory_space=pltpu.VMEM)
SMEM = pl.BlockSpec(memory_space=pltpu.SMEM)
MIB = 2**20


def params(mib):
    return pltpu.CompilerParams(vmem_limit_bytes=mib * MIB)


def cost(flops, size):
    return pl.CostEstimate(flops=int(flops), bytes_accessed=int(size), transcendentals=0)


def from_behind(value, axis, steps):
    count = lax.axis_size(axis)
    first, last = (max(0, -steps), min(count, count - steps))
    return lax.ppermute(value, axis, [(source, source + steps) for source in range(first, last)])


def swap_pieces(pieces):
    count = len(pieces)
    half = count // 2
    order = [s for pair in zip(range(half, count), [0] + list(range(1, half))) for s in pair if s]
    received = list(pieces)
    for s in order:
        received[s] = lax.ppermute(pieces[s], "mode", [(i, i ^ s) for i in range(count)])
    return received


def exchange(pieces):
    if len(pieces) == 1:
        return [lax.all_to_all(pieces[0], "mode", split_axis=0, concat_axis=0, tiled=True)]
    return swap_pieces(pieces)


def each_piece(me, refs):
    if len(refs) == 1:
        return [(owner, refs[0].at[owner]) for owner in range(refs[0].shape[0])]
    return [(me ^ s, ref) for s, ref in enumerate(refs)]


def part_of(owner, size):
    return pl.ds(owner * size if isinstance(owner, int) else pl.multiple_of(owner * size, size), size)


def pieces_shape(count, whole, shape):
    if whole:
        return [jax.ShapeDtypeStruct((count,) + shape, F32)]
    return [jax.ShapeDtypeStruct(shape, F32)] * count


def pieces_specs(shapes, first, planes):
    specs = []
    for array in shapes:
        lead = array.shape[:-4]
        zeros = (0,) * len(lead)
        block = lead + (1,) + array.shape[-3:]
        specs.append(pl.BlockSpec(block, lambda i, zeros=zeros: zeros + (jnp.clip(i - first, 0, planes - 1), 0, 0, 0)))
    return specs


def split(value):
    high = value.astype(BF16)
    return high, (value - high.astype(F32)).astype(BF16)


def prepare_kernel(pattern_ref, blocks_ref, field_ref, dense_ref, weights_ref):
    fields, row_blocks, block, stored = blocks_ref.shape
    modes = row_blocks * block
    lane = lax.broadcasted_iota(jnp.int32, (block, modes), 1)

    def one_field(k, carry):
        for r in range(row_blocks):
            value = blocks_ref[k, r]
            value = jnp.concatenate([value, jnp.zeros((block, modes - stored), F32)], axis=1)
            total = None
            for c in range(stored // block):
                part = jnp.where((lane >= c * block) & (lane < (c + 1) * block), value, 0.0)
                shift = lax.rem(pattern_ref[k, r, c] - c + row_blocks, row_blocks) * block
                part = pltpu.roll(part, shift, 1)
                total = part if total is None else total + part
            high, low = split(total)
            rows = pl.ds(pl.multiple_of(k * modes + r * block, block), block)
            dense_ref[rows, 0:modes] = high
            dense_ref[rows, modes : 2 * modes] = low
            dense_ref[rows, 2 * modes :] = high
        return carry

    lax.fori_loop(0, fields, one_field, 0)
    for z in range(weights_ref.shape[0]):
        weights_ref[z] = jnp.swapaxes(field_ref[:, z], 0, 1)


def prepare(triple_blocks, block_pattern, coefficient_fields):
    fields, row_blocks, block, _ = triple_blocks.shape
    modes = row_blocks * block
    _, depth, rows, width = coefficient_fields.shape
    return pl.pallas_call(
        prepare_kernel,
        in_specs=[SMEM, VMEM, VMEM],
        out_specs=[VMEM, VMEM],
        out_shape=[
            jax.ShapeDtypeStruct((fields * modes, 3 * modes), BF16),
            jax.ShapeDtypeStruct((depth, rows, fields, width), F32),
        ],
        compiler_params=params(16),
        cost_estimate=cost(3e9, 4 * MIB),
        name="prepare",
    )(block_pattern, triple_blocks, coefficient_fields)


def pack_kernel(count, chunks, me_ref, field_ref, *refs):
    me = me_ref[0]
    step = pl.program_id(0)
    rows = field_ref.shape[2] // count
    refs = list(refs)
    first = 0
    for planes, number in chunks:

        @pl.when((step >= first) & (step < first + planes))
        def _(outs=[refs.pop(0) for _ in range(number)]):
            for owner, out in each_piece(me, outs):
                own = field_ref[:, 0, part_of(owner, rows), :]
                out[0, :rows] = jnp.swapaxes(own, 0, 1)
                ahead = field_ref[:, 0, part_of(after(owner, count), rows), :][:, 0]
                out[0, rows] = jnp.where(owner < count - 1, ahead, 0.0)

        first += planes


def after(owner, count):
    return min(owner + 1, count - 1) if isinstance(owner, int) else jnp.minimum(owner + 1, count - 1)


def pack(me, field, chunks, count):
    modes, _, height, width = field.shape
    rows = height // count
    order = [plane for planes, _ in chunks for plane in planes]

    def plane_of(i):
        value = order[-1]
        for j, plane in enumerate(order[:-1]):
            value = jnp.where(i == j, plane, value)
        return (0, value, 0, 0)

    out_specs, out_shape, plan, first = [], [], [], 0
    for planes, whole in chunks:
        shapes = pieces_shape(count, whole, (len(planes), rows + 1, modes, width))
        out_specs += pieces_specs(shapes, first, len(planes))
        out_shape += shapes
        plan.append((len(planes), len(shapes)))
        first += len(planes)
    pieces = pl.pallas_call(
        functools.partial(pack_kernel, count, plan),
        grid=(len(order),),
        in_specs=[SMEM, pl.BlockSpec((modes, 1, height, width), plane_of)],
        out_specs=out_specs,
        out_shape=out_shape,
        compiler_params=params(16),
        cost_estimate=cost(0, 8 * len(order) * modes * height * width),
        name="pack",
    )(me, field)
    pieces = list(pieces)
    return [[pieces.pop(0) for _ in range(number)] for _, number in plan]


def edges_kernel(number, picks, me_ref, *refs):
    me = me_ref[0]
    ins, outs = refs[:number], refs[number:]
    rows = outs[0].shape[0]
    for out, index in zip(outs, picks):
        for owner, ref in each_piece(me, ins):
            out[:, part_of(owner, ref.shape[-2]), :] = ref[index, :rows]


def edges(me, received, picks, count):
    rows, size, width = received[0].shape[-3:]
    shape = jax.ShapeDtypeStruct((rows - 1, size * count, width), F32)
    return pl.pallas_call(
        functools.partial(edges_kernel, len(received), picks),
        in_specs=[SMEM] + [VMEM] * len(received),
        out_specs=[VMEM] * len(picks),
        out_shape=[shape] * len(picks),
        compiler_params=params(16),
        cost_estimate=cost(0, 16 * rows * size * count * width),
        name="edges",
    )(me, *received)


def ahead_x(value):
    width = value.shape[-1]
    lane = lax.broadcasted_iota(jnp.int32, value.shape, 1)
    return jnp.where(lane == width - 1, 0.0, pltpu.roll(value, width - 1, 1))


def behind_x(value):
    lane = lax.broadcasted_iota(jnp.int32, value.shape, 1)
    return jnp.where(lane == 0, 0.0, pltpu.roll(value, 1, 1))


def couple(c_ref, rhs_ref, groups, weights, per_step):
    flat = [gradient for group in groups for gradient in group]
    owner = [r for r, group in enumerate(groups) for _ in group]
    modes, width = flat[0].shape
    for i, gradient in enumerate(flat):
        high, low = split(gradient)
        lanes = slice(i * width, (i + 1) * width)
        rhs_ref[0:modes, lanes] = high
        rhs_ref[modes : 2 * modes, lanes] = high
        rhs_ref[2 * modes :, lanes] = low
    rhs = rhs_ref[:, : len(flat) * width]
    fields = c_ref.shape[0] // modes
    totals = [None] * len(flat)
    for k0 in range(0, fields, per_step):
        product = jnp.dot(c_ref[k0 * modes : (k0 + per_step) * modes, :], rhs, preferred_element_type=F32)
        for k in range(per_step):
            for i in range(len(flat)):
                part = product[k * modes : (k + 1) * modes, i * width : (i + 1) * width]
                part = part * weights[owner[i]][k0 + k : k0 + k + 1, :]
                totals[i] = part if totals[i] is None else totals[i] + part
    return totals


def flux_kernel(plan, me_ref, c_ref, *refs):
    tasks, sources, weights, sums_in, final, number_out, carried = plan
    me = me_ref[0]
    refs = list(refs)
    weight_refs = [refs.pop(0) for _ in range(1 + max(array for array, _ in weights.values()))]
    ins = {plane: [refs.pop(0) for _ in range(number)] for plane, (number, _) in sources.items()}
    sums = {plane: [refs.pop(0) for _ in range(number)] for plane, number in sums_in.items()}
    outs = [refs.pop(0) for _ in range(number_out)]
    goes_on = {plane: refs.pop(0) for plane in carried}
    planes_ref, rhs_ref = refs.pop(0), refs.pop(0)
    total = dict(goes_on)
    for plane in final:
        total[plane] = refs.pop(0)
    _, full_rows, modes, width = planes_ref.shape
    rows = full_rows - 1
    slot = {}
    for plane, group in ins.items():
        slot[plane] = len(slot)
        if len(group[0].shape) == 3:
            planes_ref[slot[plane], :rows] = group[0][...]
        else:
            for owner, ref in each_piece(me, group):
                planes_ref[slot[plane], :, part_of(owner, ref.shape[-2]), :] = ref[sources[plane][1]]
    for plane, ref in total.items():
        if plane in sums:
            ref[...] = functools.reduce(lambda left, right: left + right, [array[...] for array in sums[plane]])
        else:
            ref[...] = jnp.zeros_like(ref)

    def weight(plane, y):
        array, index = weights[plane]
        return weight_refs[array][index, y]

    for plane, directions in tasks:
        per_step = 2

        def step(i, carry, plane=plane, directions=directions):
            groups = []
            for j in range(per_step):
                y = per_step * i + j
                here = planes_ref[slot[plane], y]
                group = []
                if "x" in directions:
                    group.append(ahead_x(here) - here)
                if "y" in directions:
                    group.append(planes_ref[slot[plane], y + 1] - here)
                if "z" in directions:
                    group.append(planes_ref[slot[plane + 1], y] - here)
                groups.append(group)
            fluxes = couple(c_ref, rhs_ref, groups, [weight(plane, per_step * i + j) for j in range(per_step)], 4)
            here = total.get(plane)
            after = total.get(plane + 1)
            for j in range(per_step):
                y = per_step * i + j
                change = None
                for direction in directions:
                    flux = fluxes.pop(0)
                    part = behind_x(flux) - flux if direction == "x" else -flux
                    change = part if change is None else change + part
                    if direction == "y":
                        here[y + 1] += flux
                    if direction == "z" and after is not None:
                        after[y] += flux
                if here is not None:
                    here[y] += change
            return carry

        lax.fori_loop(0, rows // per_step, step, 0)
    for owner, out in each_piece(me, outs):
        for z, plane in enumerate(final):
            out[z] = total[plane][:, part_of(owner, out.shape[-2]), :]


def fluxes(me, dense, weight_arrays, tasks, sources, weights, sums, final, whole, carried, count):
    rows, fields, width = weight_arrays[0].shape[1:]
    modes = dense.shape[1] // 3
    size = modes // count
    out_shape = pieces_shape(count, whole, (len(final), rows + 1, size, width)) if final else []
    number_out = len(out_shape)
    numbers = {p: len(a) for p, a in sums.items()}
    plan = (tasks, {p: (len(a), i) for p, (a, i) in sources.items()}, weights, numbers, final, number_out, carried)
    args = list(weight_arrays) + [array for arrays, _ in sources.values() for array in arrays]
    args += [array for arrays in sums.values() for array in arrays]
    plane_sum = (rows + 1, modes, width)
    out_shape = out_shape + [jax.ShapeDtypeStruct(plane_sum, F32)] * len(carried)
    widest = max(len(directions) for _, directions in tasks)
    scratch = [pltpu.VMEM((len(sources),) + plane_sum, F32), pltpu.VMEM((3 * modes, 2 * widest * width), BF16)]
    scratch += [pltpu.VMEM(plane_sum, F32)] * len(final)
    units = rows * sum(len(directions) for _, directions in tasks)
    results = pl.pallas_call(
        functools.partial(flux_kernel, plan),
        in_specs=[SMEM, VMEM] + [VMEM] * len(args),
        out_specs=[VMEM] * len(out_shape),
        out_shape=out_shape,
        scratch_shapes=scratch,
        compiler_params=params(32),
        cost_estimate=cost(units * 2 * dense.shape[0] * 4 * modes * width, 8 * MIB),
        name="fluxes_" + "_".join(f"{plane}{directions}" for plane, directions in tasks),
    )(me, dense, *args)
    return results[:number_out], dict(zip(carried, results[number_out:]))


def unpack_kernel(count, chunks, me_ref, *refs):
    me = me_ref[0]
    step = pl.program_id(0)
    refs = list(refs)
    out = refs.pop()
    first = 0
    for planes, number in chunks:

        @pl.when((step >= first) & (step < first + planes))
        def _(ins=[refs.pop(0) for _ in range(number)]):
            for owner, ref in each_piece(me, ins):
                rows = ref.shape[-3] - 1
                out[:, 0, part_of(owner, rows), :] = jnp.swapaxes(ref[0, :rows], 0, 1)
            for owner, ref in each_piece(me, ins):
                there = part_of(after(owner, count), rows)
                added = jnp.where(owner < count - 1, ref[0, rows], 0.0)[:, None, :]
                value = out[:, 0, there, :]
                row = lax.broadcasted_iota(jnp.int32, value.shape, 1)
                out[:, 0, there, :] = value + jnp.where(row == 0, added, 0.0)

        first += planes


def unpack(me, received, chunks, shape, count):
    modes, depth, height, width = shape
    in_specs, args, plan, first = [SMEM], [me], [], 0
    for planes, pieces in zip(chunks, received):
        in_specs += pieces_specs(pieces, first, len(planes))
        args += list(pieces)
        plan.append((len(planes), len(pieces)))
        first += len(planes)
    return pl.pallas_call(
        functools.partial(unpack_kernel, count, plan),
        grid=(depth,),
        in_specs=in_specs,
        out_specs=pl.BlockSpec((modes, 1, height, width), lambda i: (0, i, 0, 0)),
        out_shape=jax.ShapeDtypeStruct(shape, F32),
        compiler_params=params(16),
        cost_estimate=cost(0, 8 * depth * modes * height * width),
        name="unpack",
    )(*args)


WHOLE = (False, True, False, True)


def body(field, coefficient_fields, triple_blocks, block_pattern):
    count = lax.axis_size("mode")
    depth = field.shape[1]
    top = depth - 1
    me = lax.axis_index("mode").astype(jnp.int32).reshape(1)

    outer, inner = (top, 0), tuple(range(1, top))
    sent_outer, sent_inner = pack(me, field, ((outer, WHOLE[0]), (inner, WHOLE[1])), count)
    sent_outer = exchange(sent_outer)
    dense, weights = prepare(triple_blocks, block_pattern, coefficient_fields)
    sent_inner = exchange(sent_inner)
    (lowest,) = edges(me, sent_outer, (1,), count)
    above = from_behind(lowest, "slab", -1)

    arrays = {0: (sent_outer, 1), top: (sent_outer, 0), depth: ([above], 0)}
    for i, plane in enumerate(inner):
        arrays[plane] = (sent_inner, i)

    def add(tasks, sums, final, whole, carried):
        needed = sorted({p for p, _ in tasks} | {p + 1 for p, directions in tasks if "z" in directions})
        where = {p: (0, p) for p, _ in tasks}
        return fluxes(me, dense, [weights], tasks, {p: arrays[p] for p in needed}, where, sums, final, whole, carried, count)

    half = depth // 2
    _, early = add(((0, "xy"), (top, "xy")), {}, (), False, (0, top))
    _, last = add(((top, "z"),), {top: [early[top]]}, (), False, (top, depth))
    below = from_behind(last[depth], "slab", 1)
    tasks = ((0, "z"),) + tuple((p, "xyz") for p in range(1, half))
    pieces, carry = add(tasks, {0: [early[0], below]}, tuple(range(half)), WHOLE[2], (half,))
    back_first = exchange(pieces)
    tasks = tuple((p, "xyz") for p in range(half, top))
    pieces, _ = add(tasks, {half: [carry[half]], top: [last[top]]}, tuple(range(half, depth)), WHOLE[3], ())
    back_second = exchange(pieces)
    chunks = (tuple(range(half)), tuple(range(half, depth)))
    return unpack(me, (back_first, back_second), chunks, field.shape, count)


def solution(mesh):
    in_specs = (P("mode", "slab", None, None), P(None, "slab", "mode", None), P(), P())
    out_specs = P("mode", "slab", None, None)
    return jax.shard_map(body, mesh=mesh, in_specs=in_specs, out_specs=out_specs, check_vma=False)
```

time: 716 us -> 174 us (0.24); the launches traced: 703 us -> 172 us
  other arithmetic: 267 us -> 0 us
  blocking collectives: 141 us -> 0 us
  matrix products: 103 us -> 0 us
  waiting for transfers between devices: 134 us -> 72.5 us
  Pallas kernels: 0 us -> 42.9 us
  local copies, waits for them, and re-layouts: 45.7 us -> 11 us
  starting transfers between devices: 11.2 us -> 45.4 us
    while x4 -> x0, other arithmetic: 257 us -> none
    all_to_all x1 -> x0, blocking collectives: 141 us -> none  [body(): lax.all_to_all(flux, 'mode', split_axis=1, concat_axis=3, tiled=True)]
    all_to_all x1 -> x2, waiting for transfers between devices: 127 us -> 0.01 us  [exchange(): lax.all_to_all(pieces[0], 'mode', split_axis=0, concat_axis=0, tiled=True)]
    dot_general x5 -> x0, matrix products: 103 us -> none  [the longest x4 96.1 us: plane_step(): jnp.einsum('kij,djn->kdin', matrices, flat, precision=lax.Precision.HIGHEST)]
    ppermute x0 -> x14, waiting for transfers between devices: none -> 65.7 us  [swap_pieces(): lax.ppermute(pieces[s], 'mode', [(i, i ^ s) for i in range(count)])]
    pallas_call x0 -> x8, Pallas kernels: none -> 42.9 us  [the longest x4 35.2 us: fluxes(): pl.pallas_call(functools.partial(flux_kernel, plan), in_specs=[SMEM, VMEM...]
    ppermute x0 -> x14, starting transfers between devices: none -> 24.3 us  [swap_pieces(): lax.ppermute(pieces[s], 'mode', [(i, i ^ s) for i in range(count)])]
    all_to_all x1 -> x0, local copies, waits for them, and re-layouts: 11 us -> none  [body(): lax.all_to_all(gradient, 'mode', split_axis=3, concat_axis=1, tiled=True)]
  transfers between devices with their start and end apart: 3 -> 18, of which waited for: 3 -> 9; matrix products, arithmetic and copies ran while one was open for 3% -> 0% of each run, Pallas kernels for 0% -> 10%
where the time goes in v1:
time: 174 us; the launch traced here: 172 us
  waiting for transfers between devices  72.5 us (42%)
  starting transfers between devices  45.4 us (26%)
  Pallas kernels  42.9 us (25%)
  local copies, waits for them, and re-layouts  11 us (6%)
    ppermute x14, waiting for transfers between devices, swap_pieces(): lax.ppermute(pieces[s], 'mode', [(i, i ^ s) for i in range(count)])  65.7 us
    pallas_call x4, Pallas kernels, fluxes(): pl.pallas_call(functools.partial(flux_kernel, plan), in_specs=[SMEM, VMEM...  35.2 us
    ppermute x14, starting transfers between devices, swap_pieces(): lax.ppermute(pieces[s], 'mode', [(i, i ^ s) for i in range(count)])  24.3 us
    all_to_all x2, starting transfers between devices, exchange(): lax.all_to_all(pieces[0], 'mode', split_axis=0, concat_axis=0, tiled=True)  13.7 us
    unnamed x43, local copies, waits for them, and re-layouts  11 us
    ppermute x2, starting transfers between devices, from_behind(): lax.ppermute(value, axis, [(source, source + steps) for source in range(f...  7.44 us
    ppermute x2, waiting for transfers between devices, from_behind(): lax.ppermute(value, axis, [(source, source + steps) for source in range(f...  6.81 us
  transfers between devices with their start and end apart: 18, of which 9 were waited for; matrix products, arithmetic and copies ran while one was open for 0% of the time, Pallas kernels for 10%

profile of v1, /device:TPU:1, one launch (start us, length us, event | category | flops | bytes accessed | tf_op | source)
XLA Modules:
  0.0 172.0 jit_solution(4969424122566944950)
XLA Ops:
  1.6 2.3 %pack.1 = (f32[2,9,16,128]{3,2,1,0:T(8,128)S(1)}, f32[2,9,16,128]{3,2,1,0:T(8,128)S(1)}, f32[2,9,16,128]{3,2,1,0:T(8,128)S(1)}, f32[2,9,16,128]{3,2,1,0:T(8,128)...) custom-call(s32[1]{0:T(128)} %bitcast.me_ref, ...), custom_call_target="tpu_custom_call" | custom-call | bytes 4194304 | tf_op jit(solution)/shard_map/pack/pallas_call | solution.py:164
  4.6 6.5 %all-to-all-start = ((f32[8,2,9,16,128]{4,3,2,1,0:T(8,128)}), f32[8,2,9,16,128]{4,3,2,1,0:T(8,128)S(1)}, u32[]{:S(2)}, u32[]{:S(2)}) async-start(f32[8,2,9,16,128]{4,3,2,1,0:T(8,128)} %get-tuple-element.39), calls=%async_computation | async-start | bytes 2359296 | tf_op jit(solution)/shard_map/all_to_all | solution.py:43
  13.7 2.3 %collective-permute-start.3 = (f32[2,9,16,128]{3,2,1,0:T(8,128)}, f32[2,9,16,128]{3,2,1,0:T(8,128)S(1)}, u32[]{:S(2)}, u32[]{:S(2)}) collective-permute-start(f32[2,9,16,128]{3,2,1,0:T(8,128)} %get-tuple-element.35), channel_id=1, source_target_pairs={{0,16},{4,20},{8,24},{12,28},{16,0},{20,4},{24,8},{28,12},{1,17},{... | collective-permute-start | bytes 442376 | tf_op jit(solution)/shard_map/ppermute | solution.py:37
  17.4 6.4 %collective-permute-done.refs_2_.refs_10_.refs_1_.refs_3_ = f32[2,9,16,128]{3,2,1,0:T(8,128)S(1)} collective-permute-done((f32[2,9,16,128]{3,2,1,0:T(8,128)S(1)}, f32[2,9,16,128]{3,2,1,0:T(8,128)S(1)}, u32[]{:S(2)}, u32[]{:S(2)}) %collective-permute-start) | collective-permute-done | bytes 147488 | tf_op jit(solution)/shard_map/ppermute | solution.py:37
  23.8 3.5 %collective-permute-start.5 = (f32[2,9,16,128]{3,2,1,0:T(8,128)}, f32[2,9,16,128]{3,2,1,0:T(8,128)S(1)}, u32[]{:S(2)}, u32[]{:S(2)}) collective-permute-start(f32[2,9,16,128]{3,2,1,0:T(8,128)} %get-tuple-element.37), channel_id=1, source_target_pairs={{0,24},{4,28},{8,16},{12,20},{16,8},{20,12},{24,0},{28,4},{1,25},{... | collective-permute-start | bytes 442376 | tf_op jit(solution)/shard_map/ppermute | solution.py:37
  27.3 5.8 %collective-permute-done.1.refs_3_.refs_11_.refs_2_.refs_4_ = f32[2,9,16,128]{3,2,1,0:T(8,128)S(1)} collective-permute-done((f32[2,9,16,128]{3,2,1,0:T(8,128)S(1)}, f32[2,9,16,128]{3,2,1,0:T(8,128)S(1)}, u32[]{:S(2)}, u32[]{:S(2)}) %collective-permute-start.1) | collective-permute-done | bytes 147488 | tf_op jit(solution)/shard_map/ppermute | solution.py:37
  33.1 3.6 %collective-permute-start.6 = (f32[2,9,16,128]{3,2,1,0:T(8,128)}, f32[2,9,16,128]{3,2,1,0:T(8,128)S(1)}, u32[]{:S(2)}, u32[]{:S(2)}) collective-permute-start(f32[2,9,16,128]{3,2,1,0:T(8,128)} %copy-done.5), channel_id=1, source_target_pairs={{0,28},{4,24},{8,20},{12,16},{16,12},{20,8},{24,4},{28,0},{1,29},{... | collective-permute-start | bytes 442376 | tf_op jit(solution)/shard_map/ppermute | solution.py:37
  37.6 2.9 %prepare.1 = (bf16[2048,384]{1,0:T(8,128)(2,1)S(1)}, f32[4,8,16,128]{3,2,1,0:T(8,128)S(1)}) custom-call(s32[16,4,2]{2,1,0:T(4,128)S(1)} %copy.5.pattern_ref, f32[16,4,32,64]{3,2,1,0:T(8,128)S(1)} %copy-done.1, f32[16,4,8,128]{3,2,1,0:T(8,128)S(1)} %copy-done.2), custom_call_target="tpu_custom_call" | custom-call | flops 3000000000 | bytes 4194304 | tf_op jit(solution)/shard_map/prepare/pallas_call | solution.py:109
  40.6 14.0 %collective-permute-done.3.refs_5_.refs_13_.refs_4_.refs_6_ = f32[2,9,16,128]{3,2,1,0:T(8,128)S(1)} collective-permute-done((f32[2,9,16,128]{3,2,1,0:T(8,128)}, f32[2,9,16,128]{3,2,1,0:T(8,128)S(1)}, u32[]{:S(2)}, u32[]{:S(2)}) %collective-permute-start.3) | collective-permute-done | bytes 147488 | tf_op jit(solution)/shard_map/ppermute | solution.py:37
  54.6 4.4 %collective-permute-done.4.refs_6_.refs_14_.refs_5_.refs_7_ = f32[2,9,16,128]{3,2,1,0:T(8,128)S(1)} collective-permute-done((f32[2,9,16,128]{3,2,1,0:T(8,128)}, f32[2,9,16,128]{3,2,1,0:T(8,128)S(1)}, u32[]{:S(2)}, u32[]{:S(2)}) %collective-permute-start.4) | collective-permute-done | bytes 147488 | tf_op jit(solution)/shard_map/ppermute | solution.py:37
  59.0 4.4 %collective-permute-start.7 = (f32[8,128,128]{2,1,0:T(8,128)S(1)}, f32[8,128,128]{2,1,0:T(8,128)S(1)}, u32[]{:S(2)}, u32[]{:S(2)}) collective-permute-start(f32[8,128,128]{2,1,0:T(8,128)S(1)} %edges.1), channel_id=1, source_target_pairs={{1,0},{2,1},{3,2},{5,4},{6,5},{7,6},{9,8},{10,9},{11,10},{13,12},{... | collective-permute-start | bytes 1572872 | tf_op jit(solution)/shard_map/ppermute | solution.py:28
  63.4 11.7 %fluxes_0xy_3xy.1 = (f32[9,128,128]{2,1,0:T(8,128)S(1)}, f32[9,128,128]{2,1,0:T(8,128)S(1)}) custom-call(s32[1]{0:T(128)} %bitcast.me_ref, bf16[2048,384]{1,0:T(8,128)(2,1)S(1)} %get-tuple-element.29.c_ref, f32[4,8,16,128]{3,2,1,0:T(8,128)S(1)} %get-tuple-element.30.refs_0_, f32[2,9,16,128]{3,2,1,0:T(8,128)S(1)} %get-tuple-element.31.refs_1_.refs_9_.refs_0_.refs_2_, ...), custom_call_target="tpu_custom_call" | custom-call | flops 8589934592 | bytes 8388608 | tf_op jit(solution)/shard_map/fluxes_0xy_3xy/pallas_call | solution.py:324
  76.0 3.3 %fluxes_3z.1 = (f32[9,128,128]{2,1,0:T(8,128)S(1)}, f32[9,128,128]{2,1,0:T(8,128)S(1)}) custom-call(s32[1]{0:T(128)} %bitcast.me_ref, bf16[2048,384]{1,0:T(8,128)(2,1)S(1)} %get-tuple-element.29.c_ref, f32[4,8,16,128]{3,2,1,0:T(8,128)S(1)} %get-tuple-element.30.refs_0_, f32[2,9,16,128]{3,2,1,0:T(8,128)S(1)} %get-tuple-element.31.refs_1_.refs_9_.refs_0_.refs_2_, ...), custom_call_target="tpu_custom_call" | custom-call | flops 2147483648 | bytes 8388608 | tf_op jit(solution)/shard_map/fluxes_3z/pallas_call | solution.py:324
  80.1 3.0 %collective-permute-start.8 = (f32[9,128,128]{2,1,0:T(8,128)S(1)}, f32[9,128,128]{2,1,0:T(8,128)S(1)}, u32[]{:S(2)}, u32[]{:S(2)}) collective-permute-start(f32[9,128,128]{2,1,0:T(8,128)S(1)} %get-tuple-element.42), channel_id=1, source_target_pairs={{0,1},{1,2},{2,3},{4,5},{5,6},{6,7},{8,9},{9,10},{10,11},{12,13},{... | collective-permute-start | bytes 1769480 | tf_op jit(solution)/shard_map/ppermute | solution.py:28
  83.1 6.8 %collective-permute-done.8.refs_12_ = f32[9,128,128]{2,1,0:T(8,128)S(1)} collective-permute-done((f32[9,128,128]{2,1,0:T(8,128)S(1)}, f32[9,128,128]{2,1,0:T(8,128)S(1)}, u32[]{:S(2)}, u32[]{:S(2)}) %collective-permute-start.8) | collective-permute-done | bytes 589856 | tf_op jit(solution)/shard_map/ppermute | solution.py:28
  93.4 11.2 %fluxes_0z_1xyz.1 = (f32[2,9,16,128]{3,2,1,0:T(8,128)S(1)}, f32[2,9,16,128]{3,2,1,0:T(8,128)S(1)}, f32[2,9,16,128]{3,2,1,0:T(8,128)S(1)}, f32[2,9,16,128]{3,2,1,...) custom-call(s32[1]{0:T(128)} %bitcast.me_ref, ...), custom_call_target="tpu_custom_call" | custom-call | flops 8589934592 | bytes 8388608 | tf_op jit(solution)/shard_map/fluxes_0z_1xyz/pallas_call | solution.py:324
  107.2 9.1 %fluxes_2xyz.1 = f32[8,2,9,16,128]{4,3,2,1,0:T(8,128)} custom-call(s32[1]{0:T(128)} %bitcast.me_ref, bf16[2048,384]{1,0:T(8,128)(2,1)S(1)} %copy-done.13, f32[4,8,16,128]{3,2,1,0:T(8,128)S(1)} %copy-done.17, f32[8,2,9,16,128]{4,3,2,1,0:T(8,128)S(1)} %all-to-all-done.refs_9_.refs_10_.refs_1_, ...), custom_call_target="tpu_custom_call" | custom-call | flops 6442450944 | bytes 8388608 | tf_op jit(solution)/shard_map/fluxes_2xyz/pallas_call | solution.py:324
  116.3 7.2 %all-to-all-start.1 = ((f32[8,2,9,16,128]{4,3,2,1,0:T(8,128)}), f32[8,2,9,16,128]{4,3,2,1,0:T(8,128)S(1)}, u32[]{:S(2)}, u32[]{:S(2)}) async-start(f32[8,2,9,16,128]{4,3,2,1,0:T(8,128)} %fluxes_2xyz.1), calls=%async_computation.1 | async-start | bytes 2359296 | tf_op jit(solution)/shard_map/all_to_all | solution.py:43
  129.7 5.4 %collective-permute-done.9.refs_1_ = f32[2,9,16,128]{3,2,1,0:T(8,128)S(1)} collective-permute-done((f32[2,9,16,128]{3,2,1,0:T(8,128)S(1)}, f32[2,9,16,128]{3,2,1,0:T(8,128)S(1)}, u32[]{:S(2)}, u32[]{:S(2)}) %collective-permute-start.9) | collective-permute-done | bytes 147488 | tf_op jit(solution)/shard_map/ppermute | solution.py:37
  135.7 10.7 %collective-permute-done.10.refs_2_ = f32[2,9,16,128]{3,2,1,0:T(8,128)S(1)} collective-permute-done((f32[2,9,16,128]{3,2,1,0:T(8,128)S(1)}, f32[2,9,16,128]{3,2,1,0:T(8,128)S(1)}, u32[]{:S(2)}, u32[]{:S(2)}) %collective-permute-start.10) | collective-permute-done | bytes 147488 | tf_op jit(solution)/shard_map/ppermute | solution.py:37
  146.4 4.2 %collective-permute-start.15 = (f32[2,9,16,128]{3,2,1,0:T(8,128)S(1)}, f32[2,9,16,128]{3,2,1,0:T(8,128)S(1)}, u32[]{:S(2)}, u32[]{:S(2)}) collective-permute-start(f32[2,9,16,128]{3,2,1,0:T(8,128)S(1)} %get-tuple-element.50), channel_id=1, source_target_pairs={{0,28},{4,24},{8,20},{12,16},{16,12},{20,8},{24,4},{28,0},{1,29},{... | collective-permute-start | bytes 442376 | tf_op jit(solution)/shard_map/ppermute | solution.py:37
  150.6 16.0 %collective-permute-done.12.refs_4_ = f32[2,9,16,128]{3,2,1,0:T(8,128)S(1)} collective-permute-done((f32[2,9,16,128]{3,2,1,0:T(8,128)S(1)}, f32[2,9,16,128]{3,2,1,0:T(8,128)S(1)}, u32[]{:S(2)}, u32[]{:S(2)}) %collective-permute-start.12) | collective-permute-done | bytes 147488 | tf_op jit(solution)/shard_map/ppermute | solution.py:37
  166.5 3.1 %collective-permute-done.13.refs_5_ = f32[2,9,16,128]{3,2,1,0:T(8,128)S(1)} collective-permute-done((f32[2,9,16,128]{3,2,1,0:T(8,128)S(1)}, f32[2,9,16,128]{3,2,1,0:T(8,128)S(1)}, u32[]{:S(2)}, u32[]{:S(2)}) %collective-permute-start.13) | collective-permute-done | bytes 147488 | tf_op jit(solution)/shard_map/ppermute | solution.py:37
  169.6 2.4 %unpack.1 = f32[16,4,64,128]{3,2,1,0:T(8,128)} custom-call(s32[1]{0:T(128)} %bitcast.me_ref, f32[2,9,16,128]{3,2,1,0:T(8,128)S(1)} %get-tuple-element.43.refs_0_, f32[2,9,16,128]{3,2,1,0:T(8,128)S(1)} %collective-permute-done.9.refs_1_, f32[2,9,16,128]{3,2,1,0:T(8,128)S(1)} %collective-permute-done.10.refs_2_, ...), custom_call_target="tpu_custom_call" | custom-call | bytes 4194304 | tf_op jit(solution)/shard_map/unpack/pallas_call | solution.py:368
  (63 shorter events, 21.8 us)
Async XLA Ops:
  4.6 12.7 %copy-start.20 = (s32[16,4,2]{0,2,1:T(2,128)S(1)}, s32[16,4,2]{0,2,1:T(2,128)}, u32[]{:S(2)}) copy-start(s32[16,4,2]{0,2,1:T(2,128)} %param.7) | copy-start | bytes 1540
  4.6 32.1 %copy-start.1 = (f32[16,4,32,64]{3,2,1,0:T(8,128)S(1)}, f32[16,4,32,64]{3,2,1,0:T(8,128)}, u32[]{:S(2)}) copy-start(f32[16,4,32,64]{3,2,1,0:T(8,128)} %blocks_ref.1) | copy-start | bytes 1572868
  4.6 85.4 %all-to-all-start = ((f32[8,2,9,16,128]{4,3,2,1,0:T(8,128)}), f32[8,2,9,16,128]{4,3,2,1,0:T(8,128)S(1)}, u32[]{:S(2)}, u32[]{:S(2)}) async-start(f32[8,2,9,16,128]{4,3,2,1,0:T(8,128)} %get-tuple-element.39), calls=%async_computation | async-start | bytes 2359296 | tf_op jit(solution)/shard_map/all_to_all | solution.py:43
  11.1 12.7 %collective-permute-start = (f32[2,9,16,128]{3,2,1,0:T(8,128)S(1)}, f32[2,9,16,128]{3,2,1,0:T(8,128)S(1)}, u32[]{:S(2)}, u32[]{:S(2)}) collective-permute-start(f32[2,9,16,128]{3,2,1,0:T(8,128)S(1)} %get-tuple-element.32), channel_id=1, source_target_pairs={{0,4},{4,0},{8,12},{12,8},{16,20},{20,16},{24,28},{28,24},{1,5},{5... | collective-permute-start | bytes 442376 | tf_op jit(solution)/shard_map/ppermute | solution.py:37
  12.5 20.6 %collective-permute-start.1 = (f32[2,9,16,128]{3,2,1,0:T(8,128)S(1)}, f32[2,9,16,128]{3,2,1,0:T(8,128)S(1)}, u32[]{:S(2)}, u32[]{:S(2)}) collective-permute-start(f32[2,9,16,128]{3,2,1,0:T(8,128)S(1)} %get-tuple-element.33), channel_id=1, source_target_pairs={{0,8},{4,12},{8,0},{12,4},{16,24},{20,28},{24,16},{28,20},{1,9},{5... | collective-permute-start | bytes 442376 | tf_op jit(solution)/shard_map/ppermute | solution.py:37
  13.7 26.9 %collective-permute-start.2 = (f32[2,9,16,128]{3,2,1,0:T(8,128)}, f32[2,9,16,128]{3,2,1,0:T(8,128)S(1)}, u32[]{:S(2)}, u32[]{:S(2)}) collective-permute-start(f32[2,9,16,128]{3,2,1,0:T(8,128)} %get-tuple-element.34), channel_id=1, source_target_pairs={{0,12},{4,8},{8,4},{12,0},{16,28},{20,24},{24,20},{28,16},{1,13},{... | collective-permute-start | bytes 442376 | tf_op jit(solution)/shard_map/ppermute | solution.py:37
  13.7 40.8 %collective-permute-start.3 = (f32[2,9,16,128]{3,2,1,0:T(8,128)}, f32[2,9,16,128]{3,2,1,0:T(8,128)S(1)}, u32[]{:S(2)}, u32[]{:S(2)}) collective-permute-start(f32[2,9,16,128]{3,2,1,0:T(8,128)} %get-tuple-element.35), channel_id=1, source_target_pairs={{0,16},{4,20},{8,24},{12,28},{16,0},{20,4},{24,8},{28,12},{1,17},{... | collective-permute-start | bytes 442376 | tf_op jit(solution)/shard_map/ppermute | solution.py:37
  16.1 42.9 %collective-permute-start.4 = (f32[2,9,16,128]{3,2,1,0:T(8,128)}, f32[2,9,16,128]{3,2,1,0:T(8,128)S(1)}, u32[]{:S(2)}, u32[]{:S(2)}) collective-permute-start(f32[2,9,16,128]{3,2,1,0:T(8,128)} %get-tuple-element.36), channel_id=1, source_target_pairs={{0,20},{4,16},{8,28},{12,24},{16,4},{20,0},{24,12},{28,8},{1,21},{... | collective-permute-start | bytes 442376 | tf_op jit(solution)/shard_map/ppermute | solution.py:37
  23.8 35.2 %collective-permute-start.5 = (f32[2,9,16,128]{3,2,1,0:T(8,128)}, f32[2,9,16,128]{3,2,1,0:T(8,128)S(1)}, u32[]{:S(2)}, u32[]{:S(2)}) collective-permute-start(f32[2,9,16,128]{3,2,1,0:T(8,128)} %get-tuple-element.37), channel_id=1, source_target_pairs={{0,24},{4,28},{8,16},{12,20},{16,8},{20,12},{24,0},{28,4},{1,25},{... | collective-permute-start | bytes 442376 | tf_op jit(solution)/shard_map/ppermute | solution.py:37
  33.1 25.8 %collective-permute-start.6 = (f32[2,9,16,128]{3,2,1,0:T(8,128)}, f32[2,9,16,128]{3,2,1,0:T(8,128)S(1)}, u32[]{:S(2)}, u32[]{:S(2)}) collective-permute-start(f32[2,9,16,128]{3,2,1,0:T(8,128)} %copy-done.5), channel_id=1, source_target_pairs={{0,28},{4,24},{8,20},{12,16},{16,12},{20,8},{24,4},{28,0},{1,29},{... | collective-permute-start | bytes 442376 | tf_op jit(solution)/shard_map/ppermute | solution.py:37
  40.6 35.4 %copy-start.12 = (bf16[2048,384]{1,0:T(8,128)(2,1)}, bf16[2048,384]{1,0:T(8,128)(2,1)S(1)}, u32[]{:S(2)}) copy-start(bf16[2048,384]{1,0:T(8,128)(2,1)S(1)} %get-tuple-element.29.c_ref) | copy-start | bytes 4718596
  40.6 35.4 %copy-start.16 = (f32[4,8,16,128]{3,2,1,0:T(8,128)}, f32[4,8,16,128]{3,2,1,0:T(8,128)S(1)}, u32[]{:S(2)}) copy-start(f32[4,8,16,128]{3,2,1,0:T(8,128)S(1)} %get-tuple-element.30.refs_0_) | copy-start | bytes 786436
  59.0 17.0 %collective-permute-start.7 = (f32[8,128,128]{2,1,0:T(8,128)S(1)}, f32[8,128,128]{2,1,0:T(8,128)S(1)}, u32[]{:S(2)}, u32[]{:S(2)}) collective-permute-start(f32[8,128,128]{2,1,0:T(8,128)S(1)} %edges.1), channel_id=1, source_target_pairs={{1,0},{2,1},{3,2},{5,4},{6,5},{7,6},{9,8},{10,9},{11,10},{13,12},{... | collective-permute-start | bytes 1572872 | tf_op jit(solution)/shard_map/ppermute | solution.py:28
  80.1 9.8 %collective-permute-start.8 = (f32[9,128,128]{2,1,0:T(8,128)S(1)}, f32[9,128,128]{2,1,0:T(8,128)S(1)}, u32[]{:S(2)}, u32[]{:S(2)}) collective-permute-start(f32[9,128,128]{2,1,0:T(8,128)S(1)} %get-tuple-element.42), channel_id=1, source_target_pairs={{0,1},{1,2},{2,3},{4,5},{5,6},{6,7},{8,9},{9,10},{10,11},{12,13},{... | collective-permute-start | bytes 1769480 | tf_op jit(solution)/shard_map/ppermute | solution.py:28
  93.4 13.8 %copy-start.15 = (f32[9,128,128]{2,1,0:T(8,128)S(1)}, f32[9,128,128]{2,1,0:T(8,128)}, u32[]{:S(2)}) copy-start(f32[9,128,128]{2,1,0:T(8,128)} %copy-done.14) | copy-start | bytes 1769476
  116.3 10.5 %copy-start.4 = (f32[2,9,16,128]{3,2,1,0:T(8,128)S(1)}, f32[2,9,16,128]{3,2,1,0:T(8,128)}, u32[]{:S(2)}) copy-start(f32[2,9,16,128]{3,2,1,0:T(8,128)} %copy-done.3) | copy-start | bytes 442372
  116.3 53.3 %all-to-all-start.1 = ((f32[8,2,9,16,128]{4,3,2,1,0:T(8,128)}), f32[8,2,9,16,128]{4,3,2,1,0:T(8,128)S(1)}, u32[]{:S(2)}, u32[]{:S(2)}) async-start(f32[8,2,9,16,128]{4,3,2,1,0:T(8,128)} %fluxes_2xyz.1), calls=%async_computation.1 | async-start | bytes 2359296 | tf_op jit(solution)/shard_map/all_to_all | solution.py:43
  123.5 11.6 %collective-permute-start.9 = (f32[2,9,16,128]{3,2,1,0:T(8,128)S(1)}, f32[2,9,16,128]{3,2,1,0:T(8,128)S(1)}, u32[]{:S(2)}, u32[]{:S(2)}) collective-permute-start(f32[2,9,16,128]{3,2,1,0:T(8,128)S(1)} %copy-done.11), channel_id=1, source_target_pairs={{0,4},{4,0},{8,12},{12,8},{16,20},{20,16},{24,28},{28,24},{1,5},{5... | collective-permute-start | bytes 442376 | tf_op jit(solution)/shard_map/ppermute | solution.py:37
  124.9 21.5 %collective-permute-start.10 = (f32[2,9,16,128]{3,2,1,0:T(8,128)S(1)}, f32[2,9,16,128]{3,2,1,0:T(8,128)S(1)}, u32[]{:S(2)}, u32[]{:S(2)}) collective-permute-start(f32[2,9,16,128]{3,2,1,0:T(8,128)S(1)} %copy-done.9), channel_id=1, source_target_pairs={{0,8},{4,12},{8,0},{12,4},{16,24},{20,28},{24,16},{28,20},{1,9},{5... | collective-permute-start | bytes 442376 | tf_op jit(solution)/shard_map/ppermute | solution.py:37
  126.1 24.5 %collective-permute-start.11 = (f32[2,9,16,128]{3,2,1,0:T(8,128)S(1)}, f32[2,9,16,128]{3,2,1,0:T(8,128)S(1)}, u32[]{:S(2)}, u32[]{:S(2)}) collective-permute-start(f32[2,9,16,128]{3,2,1,0:T(8,128)S(1)} %copy-done.7), channel_id=1, source_target_pairs={{0,12},{4,8},{8,4},{12,0},{16,28},{20,24},{24,20},{28,16},{1,13},{... | collective-permute-start | bytes 442376 | tf_op jit(solution)/shard_map/ppermute | solution.py:37
  126.8 39.7 %collective-permute-start.12 = (f32[2,9,16,128]{3,2,1,0:T(8,128)S(1)}, f32[2,9,16,128]{3,2,1,0:T(8,128)S(1)}, u32[]{:S(2)}, u32[]{:S(2)}) collective-permute-start(f32[2,9,16,128]{3,2,1,0:T(8,128)S(1)} %copy-done.4), channel_id=1, source_target_pairs={{0,16},{4,20},{8,24},{12,28},{16,0},{20,4},{24,8},{28,12},{1,17},{... | collective-permute-start | bytes 442376 | tf_op jit(solution)/shard_map/ppermute | solution.py:37
  128.5 41.1 %collective-permute-start.13 = (f32[2,9,16,128]{3,2,1,0:T(8,128)S(1)}, f32[2,9,16,128]{3,2,1,0:T(8,128)S(1)}, u32[]{:S(2)}, u32[]{:S(2)}) collective-permute-start(f32[2,9,16,128]{3,2,1,0:T(8,128)S(1)} %get-tuple-element.48), channel_id=1, source_target_pairs={{0,20},{4,16},{8,28},{12,24},{16,4},{20,0},{24,12},{28,8},{1,21},{... | collective-permute-start | bytes 442376 | tf_op jit(solution)/shard_map/ppermute | solution.py:37
  135.0 34.6 %collective-permute-start.14 = (f32[2,9,16,128]{3,2,1,0:T(8,128)S(1)}, f32[2,9,16,128]{3,2,1,0:T(8,128)S(1)}, u32[]{:S(2)}, u32[]{:S(2)}) collective-permute-start(f32[2,9,16,128]{3,2,1,0:T(8,128)S(1)} %get-tuple-element.49), channel_id=1, source_target_pairs={{0,24},{4,28},{8,16},{12,20},{16,8},{20,12},{24,0},{28,4},{1,25},{... | collective-permute-start | bytes 442376 | tf_op jit(solution)/shard_map/ppermute | solution.py:37
  146.4 23.2 %collective-permute-start.15 = (f32[2,9,16,128]{3,2,1,0:T(8,128)S(1)}, f32[2,9,16,128]{3,2,1,0:T(8,128)S(1)}, u32[]{:S(2)}, u32[]{:S(2)}) collective-permute-start(f32[2,9,16,128]{3,2,1,0:T(8,128)S(1)} %get-tuple-element.50), channel_id=1, source_target_pairs={{0,28},{4,24},{8,20},{12,16},{16,12},{20,8},{24,4},{28,0},{1,29},{... | collective-permute-start | bytes 442376 | tf_op jit(solution)/shard_map/ppermute | solution.py:37
  (15 other events, 36.6 us)

commit v2 on v0

v2 whole, which is shorter than its diff:
```python
import functools

import jax
import jax.numpy as jnp
from jax import lax
from jax.experimental import pallas as pl
from jax.experimental.pallas import tpu as pltpu
from jax.sharding import PartitionSpec as P

F32 = jnp.float32
BF16 = jnp.bfloat16
VMEM = pl.BlockSpec(memory_space=pltpu.VMEM)
SMEM = pl.BlockSpec(memory_space=pltpu.SMEM)
MIB = 2**20


def params(mib):
    return pltpu.CompilerParams(vmem_limit_bytes=mib * MIB)


def cost(flops, size):
    return pl.CostEstimate(flops=int(flops), bytes_accessed=int(size), transcendentals=0)


def from_behind(value, axis, steps):
    count = lax.axis_size(axis)
    first, last = (max(0, -steps), min(count, count - steps))
    return lax.ppermute(value, axis, [(source, source + steps) for source in range(first, last)])


def exchange(pieces, order):
    count = len(pieces)
    received = list(pieces)
    for s in order:
        received[s] = lax.ppermute(pieces[s], "mode", [(i, i ^ s) for i in range(count)])
    return received


def part_of(owner, size):
    return pl.ds(pl.multiple_of(owner * size, size), size)


def after(owner, count):
    return jnp.minimum(owner + 1, count - 1)


def split(value):
    high = value.astype(BF16)
    return high, (value - high.astype(F32)).astype(BF16)


def prepare_kernel(count, me_ref, pattern_ref, blocks_ref, field_ref, *outs):
    dense_refs, weights_ref = outs[:4], outs[4]
    fields, row_blocks, block, stored = blocks_ref.shape
    modes = row_blocks * block
    half = modes // 2
    lane = lax.broadcasted_iota(jnp.int32, (block, modes), 1)
    side = me_ref[0] // (count // 2)

    def one_field(k, carry):
        for j in range(row_blocks):
            rows_side, local = divmod(j, row_blocks // 2)
            r = (side ^ rows_side) * (row_blocks // 2) + local
            value = blocks_ref[k, r]
            value = jnp.concatenate([value, jnp.zeros((block, modes - stored), F32)], axis=1)
            total = None
            for c in range(stored // block):
                part = jnp.where((lane >= c * block) & (lane < (c + 1) * block), value, 0.0)
                shift = lax.rem(pattern_ref[k, r, c] - c + row_blocks, row_blocks) * block
                part = pltpu.roll(part, shift, 1)
                total = part if total is None else total + part
            total = pltpu.roll(total, side * half, 1)
            high, low = (part.astype(F32) for part in split(total))
            other_high, other_low = pltpu.roll(high, half, 1), pltpu.roll(low, half, 1)
            rows = pl.ds(pl.multiple_of(k * half + local * block, block), block)
            near = jnp.where(lane < half, high, other_low).astype(BF16), high[:, :half].astype(BF16)
            far = jnp.where(lane < half, other_high, low).astype(BF16), other_high[:, :half].astype(BF16)
            for columns_side, parts in enumerate((near, far)):
                dense_refs[2 * columns_side + rows_side][rows, 0:modes] = parts[0]
                dense_refs[2 * columns_side + rows_side][rows, modes:] = parts[1]
        return carry

    lax.fori_loop(0, fields, one_field, 0)
    for z in range(weights_ref.shape[0]):
        weights_ref[z] = jnp.swapaxes(field_ref[:, z], 0, 1)


def prepare(me, triple_blocks, block_pattern, coefficient_fields, count):
    fields, row_blocks, block, _ = triple_blocks.shape
    modes = row_blocks * block
    _, depth, rows, width = coefficient_fields.shape
    part = jax.ShapeDtypeStruct((fields * modes // 2, 3 * modes // 2), BF16)
    *parts, weights = pl.pallas_call(
        functools.partial(prepare_kernel, count),
        in_specs=[SMEM, SMEM, VMEM, VMEM],
        out_specs=[VMEM] * 5,
        out_shape=[part] * 4 + [jax.ShapeDtypeStruct((depth, rows, fields, width), F32)],
        compiler_params=params(16),
        cost_estimate=cost(1, 1),
        name="prepare",
    )(me, block_pattern, triple_blocks, coefficient_fields)
    return {(i // 2, i % 2): part for i, part in enumerate(parts)}, weights


def pack_kernel(count, me_ref, field_ref, *outs):
    me = me_ref[0]
    rows = field_ref.shape[2] // count
    for s, out in enumerate(outs):
        owner = me ^ s
        own = field_ref[:, 0, part_of(owner, rows), :]
        out[0, :rows] = jnp.swapaxes(own, 0, 1)
        ahead = field_ref[:, 0, part_of(after(owner, count), rows), :][:, 0]
        out[0, rows] = jnp.where(owner < count - 1, ahead, 0.0)


def pack(me, field, count):
    modes, depth, height, width = field.shape
    rows = height // count
    block = (1, rows + 1, modes, width)
    return pl.pallas_call(
        functools.partial(pack_kernel, count),
        grid=(depth,),
        in_specs=[SMEM, pl.BlockSpec((modes, 1, height, width), lambda i: (0, i, 0, 0))],
        out_specs=[pl.BlockSpec(block, lambda i: (i, 0, 0, 0))] * count,
        out_shape=[jax.ShapeDtypeStruct((depth,) + block[1:], F32)] * count,
        compiler_params=params(16),
        cost_estimate=cost(1, 1),
        name="pack",
    )(me, field)


def half_row(me, s, count, size):
    return part_of((me ^ s) & (count // 2 - 1), size)


def ahead_x(value):
    width = value.shape[-1]
    lane = lax.broadcasted_iota(jnp.int32, value.shape, 1)
    return jnp.where(lane == width - 1, 0.0, pltpu.roll(value, width - 1, 1))


def behind_x(value):
    lane = lax.broadcasted_iota(jnp.int32, value.shape, 1)
    return jnp.where(lane == 0, 0.0, pltpu.roll(value, 1, 1))


def edges_kernel(count, picks, me_ref, *refs):
    me = me_ref[0]
    near, far, outs = refs[: len(picks)], refs[len(picks) : len(picks) + count // 2], refs[len(picks) + count // 2 :]
    for out, own, index in zip(outs, near, picks):
        rows, modes, _ = out.shape
        out[:, : modes // 2, :] = own[...]
        for i, ref in enumerate(far):
            size = ref.shape[2]
            start = modes // 2 + ((me ^ (i + count // 2)) & (count // 2 - 1)) * size
            out[:, pl.ds(pl.multiple_of(start, size), size), :] = ref[index, :rows]


def edges(me, near, far, picks, count):
    rows, half, width = near[0].shape
    return pl.pallas_call(
        functools.partial(edges_kernel, count, picks),
        in_specs=[SMEM] + [VMEM] * (len(near) + len(far)),
        out_specs=[VMEM] * len(picks),
        out_shape=[jax.ShapeDtypeStruct((rows, 2 * half, width), F32)] * len(picks),
        compiler_params=params(16),
        cost_estimate=cost(1, 1),
        name="edges",
    )(me, *near, *far)


def couple(c_refs, rhs_ref, groups, weights, per_step):
    flat = [gradient for group in groups for gradient in group]
    owner = [r for r, group in enumerate(groups) for _ in group]
    half, width = flat[0].shape
    for i, gradient in enumerate(flat):
        high, low = split(gradient)
        lanes = slice(i * width, (i + 1) * width)
        rhs_ref[0:half, lanes] = high
        rhs_ref[half : 2 * half, lanes] = high
        rhs_ref[2 * half :, lanes] = low
    rhs = rhs_ref[:, : len(flat) * width]
    results = []
    for c_ref in c_refs:
        fields = c_ref.shape[0] // half
        totals = [None] * len(flat)
        for k0 in range(0, fields, per_step):
            product = jnp.dot(c_ref[k0 * half : (k0 + per_step) * half, :], rhs, preferred_element_type=F32)
            for k in range(per_step):
                for i in range(len(flat)):
                    part = product[k * half : (k + 1) * half, i * width : (i + 1) * width]
                    part = part * weights[owner[i]][k0 + k : k0 + k + 1, :]
                    totals[i] = part if totals[i] is None else totals[i] + part
        results.append(totals)
    return results


def flux_kernel(count, plan, me_ref, w_ref, *refs):
    tasks, dense_keys, sources, behind, sums_in, final, carried, edges = plan
    me = me_ref[0]
    refs = list(refs)
    dense = {key: refs.pop(0) for key in dense_keys}
    w_behind = refs.pop(0) if behind else None
    ins = [[refs.pop(0) for _ in range(number)] for _, _, number, _ in sources]
    sums = {key: refs.pop(0) for key in sums_in}
    outs = [refs.pop(0) for _ in range(count // 2 if final else 0)]
    total = {key: refs.pop(0) for key in carried}
    edge_refs = [refs.pop(0) for _ in edges]
    planes_ref, rhs_ref = refs.pop(0), refs.pop(0)
    for key in final:
        total[key] = refs.pop(0)
    _, full_rows, half_modes, width = planes_ref.shape
    rows = full_rows - 1
    slot = {}
    for (plane, half, _, index), group in zip(sources, ins):
        here = slot[plane, half] = len(slot)
        if len(group) == 1:
            planes_ref[here, :rows] = group[0][:, half * half_modes : (half + 1) * half_modes, :]
        else:
            for i, ref in enumerate(group):
                planes_ref[here, :, half_row(me, i + half * count // 2, count, ref.shape[2]), :] = ref[index]
    for ref, key in zip(edge_refs, edges):
        ref[...] = planes_ref[slot[key], :rows]
    for key, ref in total.items():
        ref[...] = sums[key][...] if key in sums else jnp.zeros_like(ref)

    for plane, directions, half, sides in tasks:
        per_step = 2 if len(directions) > 1 else 4

        def step(i, carry, plane=plane, directions=directions, half=half, sides=sides, per_step=per_step):
            groups, weights = [], []
            for j in range(per_step):
                y = per_step * i + j
                here = planes_ref[slot[plane, half], y]
                group = []
                if "x" in directions:
                    group.append(ahead_x(here) - here)
                if "y" in directions:
                    group.append(planes_ref[slot[plane, half], y + 1] - here)
                if "z" in directions:
                    group.append(planes_ref[slot[plane + 1, half], y] - here)
                groups.append(group)
                weights.append(w_behind[0, y] if plane < 0 else w_ref[plane, y])
            results = couple([dense[half, side] for side in sides], rhs_ref, groups, weights, 4)
            for side, fluxes in zip(sides, results):
                here = total.get((plane, side))
                above = total.get((plane + 1, side))
                for j in range(per_step):
                    y = per_step * i + j
                    change = None
                    for direction in directions:
                        flux = fluxes.pop(0)
                        part = behind_x(flux) - flux if direction == "x" else -flux
                        change = part if change is None else change + part
                        if direction == "y":
                            here[y + 1] += flux
                        if direction == "z" and above is not None:
                            above[y] += flux
                    if here is not None:
                        here[y] += change
            return carry

        lax.fori_loop(0, rows // per_step, step, 0)
    side = final[0][1] if final else 0
    for i, out in enumerate(outs):
        for z, key in enumerate(final):
            out[z] = total[key][:, half_row(me, i + side * count // 2, count, out.shape[2]), :]


def fluxes(me, dense, weights, behind, tasks, sources, sums, final, carried, count, edges=(), busy=True):
    _, rows, fields, width = weights.shape
    half_modes = dense[0, 0].shape[0] // fields
    dense_keys = tuple(sorted({(half, side) for _, _, half, sides in tasks for side in sides}))
    needed = {(p, h) for p, _, h, _ in tasks} | {(p + 1, h) for p, directions, h, _ in tasks if "z" in directions}
    needed = sorted(needed | set(edges))
    listed = tuple((p, h, len(sources[p, h][0]), sources[p, h][1]) for p, h in needed)
    plan = (tasks, dense_keys, listed, behind is not None, tuple(sums), final, carried, edges)
    args = [weights] + [dense[key] for key in dense_keys] + ([] if behind is None else [behind])
    args += [array for key in needed for array in sources[key][0]] + list(sums.values())
    whole = (rows + 1, half_modes, width)
    piece = jax.ShapeDtypeStruct((len(final), rows + 1, 2 * half_modes // count, width), F32)
    out_shape = [piece] * (count // 2 if final else 0)
    number_out = len(out_shape)
    out_shape += [jax.ShapeDtypeStruct(whole, F32)] * len(carried)
    out_shape += [jax.ShapeDtypeStruct((rows, half_modes, width), F32)] * len(edges)
    scratch = [pltpu.VMEM((len(listed),) + whole, F32), pltpu.VMEM((3 * half_modes, 6 * width), BF16)]
    scratch += [pltpu.VMEM(whole, F32)] * len(final)
    units = rows * sum(len(directions) * len(sides) for _, directions, _, sides in tasks)
    results = pl.pallas_call(
        functools.partial(flux_kernel, count, plan),
        in_specs=[SMEM] + [VMEM] * len(args),
        out_specs=[VMEM] * len(out_shape),
        out_shape=out_shape,
        scratch_shapes=scratch,
        compiler_params=params(32),
        cost_estimate=cost(busy * units * 4 * dense[0, 0].shape[0] * 2 * half_modes * width, 1),
        name="fluxes_" + "_".join(f"{p}{directions}{half}" for p, directions, half, _ in tasks),
    )(me, *args)
    sums_out = dict(zip(carried, results[number_out:]))
    return results[:number_out], sums_out, results[number_out + len(carried) :]


def unpack_kernel(count, chunks, me_ref, *refs):
    me = me_ref[0]
    step = pl.program_id(0)
    out = refs[-1]
    for c, planes in enumerate(chunks):
        chosen = functools.reduce(lambda left, right: left | right, [step == plane for plane in planes])

        @pl.when(chosen)
        def _(ins=refs[c * count : (c + 1) * count]):
            rows = ins[0].shape[1] - 1
            for s, ref in enumerate(ins):
                out[:, 0, part_of(me ^ s, rows), :] = jnp.swapaxes(ref[0, :rows], 0, 1)
            for s, ref in enumerate(ins):
                owner = me ^ s
                there = part_of(after(owner, count), rows)
                added = jnp.where(owner < count - 1, ref[0, rows], 0.0)[:, None, :]
                value = out[:, 0, there, :]
                row = lax.broadcasted_iota(jnp.int32, value.shape, 1)
                out[:, 0, there, :] = value + jnp.where(row == 0, added, 0.0)


def unpack(me, received, chunks, shape):
    modes, depth, height, width = shape
    count = len(received[0])
    in_specs, args = [SMEM], [me]
    for planes, pieces in zip(chunks, received):

        def place(i, planes=planes):
            return (functools.reduce(jnp.add, [(i >= plane).astype(jnp.int32) for plane in planes[1:]], 0), 0, 0, 0)

        in_specs += [pl.BlockSpec((1,) + pieces[0].shape[1:], place)] * count
        args += list(pieces)
    return pl.pallas_call(
        functools.partial(unpack_kernel, count, chunks),
        grid=(depth,),
        in_specs=in_specs,
        out_specs=pl.BlockSpec((modes, 1, height, width), lambda i: (0, i, 0, 0)),
        out_shape=jax.ShapeDtypeStruct(shape, F32),
        compiler_params=params(16),
        cost_estimate=cost(1, 1),
        name="unpack",
    )(*args)


def body(field, coefficient_fields, triple_blocks, block_pattern):
    count = lax.axis_size("mode")
    depth = field.shape[1]
    top = depth - 1
    me = lax.axis_index("mode").astype(jnp.int32).reshape(1)
    near, far = tuple(range(1, count // 2)), tuple(range(count // 2, count))
    forth = far[:1] + near + far[1:]

    sent = exchange(pack(me, field, count), forth)
    dense, weights = prepare(me, triple_blocks, block_pattern, coefficient_fields, count)
    weights_behind = from_behind(weights[top:], "slab", 1)
    sides = (sent[: count // 2], sent[count // 2 :])
    sources = {(p, h): (sides[h], p) for p in range(depth) for h in (0, 1)}

    def add(*args, **options):
        return fluxes(me, dense, weights, *args, count, **options)

    def keys(side):
        return tuple((p, side) for p in range(depth))

    def inside(half, to):
        return tuple((p, "xyz", half, to) for p in range(top)) + ((top, "xy", half, to),)

    def outside(to):
        return tuple((p, "z", half, to) for half in (0, 1) for p in (top, -1))

    _, sums, near_ends = add(None, inside(0, (0, 1)), sources, {}, (), keys(0) + keys(1), edges=((0, 0), (top, 0)), busy=False)
    lowest, highest = edges(me, near_ends, sides[1], (0, top), count)
    above = from_behind(lowest, "slab", -1)
    below = from_behind(highest, "slab", 1)
    for half in (0, 1):
        sources[depth, half] = ([above], 0)
        sources[-1, half] = ([below], 0)
    _, far_sums, _ = add(None, inside(1, (1,)), sources, {key: sums[key] for key in keys(1)}, (), keys(1))
    far_pieces, _, _ = add(weights_behind, outside((1,)), sources, far_sums, keys(1), ())
    near_sums = {key: sums[key] for key in keys(0)}
    near_pieces, _, _ = add(weights_behind, inside(1, (0,)) + outside((0,)), sources, near_sums, keys(0), ())
    back = exchange(list(near_pieces) + list(far_pieces), far + near)
    return unpack(me, (back,), (tuple(range(depth)),), field.shape)


def solution(mesh):
    in_specs = (P("mode", "slab", None, None), P(None, "slab", "mode", None), P(), P())
    out_specs = P("mode", "slab", None, None)
    return jax.shard_map(body, mesh=mesh, in_specs=in_specs, out_specs=out_specs, check_vma=False)
```

time: 716 us -> 140 us (0.20); the launches traced: 703 us -> 138 us
  other arithmetic: 267 us -> 0 us
  blocking collectives: 141 us -> 0 us
  matrix products: 103 us -> 0 us
  waiting for transfers between devices: 134 us -> 41.1 us
  Pallas kernels: 0 us -> 57.5 us
  local copies, waits for them, and re-layouts: 45.7 us -> 2.67 us
  starting transfers between devices: 11.2 us -> 36.3 us
    while x4 -> x0, other arithmetic: 257 us -> none
    all_to_all x1 -> x0, blocking collectives: 141 us -> none  [body(): lax.all_to_all(flux, 'mode', split_axis=1, concat_axis=3, tiled=True)]
    all_to_all x1 -> x0, waiting for transfers between devices: 127 us -> none  [body(): lax.all_to_all(gradient, 'mode', split_axis=3, concat_axis=1, tiled=True)]
    dot_general x5 -> x0, matrix products: 103 us -> none  [the longest x4 96.1 us: plane_step(): jnp.einsum('kij,djn->kdin', matrices, flat, precision=lax.Precision.HIGHEST)]
    pallas_call x0 -> x8, Pallas kernels: none -> 57.5 us  [the longest x4 48 us: fluxes(): pl.pallas_call(functools.partial(flux_kernel, count, plan), in_specs=[SME...]
    ppermute x0 -> x14, waiting for transfers between devices: none -> 41.1 us  [exchange(): lax.ppermute(pieces[s], 'mode', [(i, i ^ s) for i in range(count)])]
    ppermute x0 -> x14, starting transfers between devices: none -> 24.9 us  [exchange(): lax.ppermute(pieces[s], 'mode', [(i, i ^ s) for i in range(count)])]
    all_to_all x1 -> x0, local copies, waits for them, and re-layouts: 11 us -> none  [body(): lax.all_to_all(gradient, 'mode', split_axis=3, concat_axis=1, tiled=True)]
  transfers between devices with their start and end apart: 3 -> 17, of which waited for: 3 -> 6; matrix products, arithmetic and copies ran while one was open for 3% -> 0% of each run, Pallas kernels for 0% -> 36%
where the time goes in v2:
time: 140 us; the launch traced here: 138 us
  Pallas kernels  57.5 us (41%)
  waiting for transfers between devices  41.1 us (29%)
  starting transfers between devices  36.3 us (26%)
  local copies, waits for them, and re-layouts  2.67 us (2%)
    pallas_call x4, Pallas kernels, fluxes(): pl.pallas_call(functools.partial(flux_kernel, count, plan), in_specs=[SME...  48 us
    ppermute x14, waiting for transfers between devices, exchange(): lax.ppermute(pieces[s], 'mode', [(i, i ^ s) for i in range(count)])  41.1 us
    ppermute x14, starting transfers between devices, exchange(): lax.ppermute(pieces[s], 'mode', [(i, i ^ s) for i in range(count)])  24.9 us
    ppermute x3, starting transfers between devices, from_behind(): lax.ppermute(value, axis, [(source, source + steps) for source in range(f...  11.4 us
    pallas_call x1, Pallas kernels, prepare(): pl.pallas_call(functools.partial(prepare_kernel, count), in_specs=[SMEM,...  5.24 us
  transfers between devices with their start and end apart: 17, of which 6 were waited for; matrix products, arithmetic and copies ran while one was open for 0% of the time, Pallas kernels for 36%

profile of v2, /device:TPU:1, one launch (start us, length us, event | category | flops | bytes accessed | tf_op | source)
XLA Modules:
  0.0 137.8 jit_solution(14056516637461591624)
XLA Ops:
  0.0 1.6 %copy-done = f32[16,4,64,128]{3,2,1,0:T(8,128)S(1)} copy-done((f32[16,4,64,128]{3,2,1,0:T(8,128)S(1)}, f32[16,4,64,128]{3,2,1,0:T(8,128)}, u32[]{:S(2)}) %copy-start) | copy-done | bytes 2097176
  1.6 1.9 %pack.1 = (f32[4,9,16,128]{3,2,1,0:T(8,128)S(1)}, f32[4,9,16,128]{3,2,1,0:T(8,128)S(1)}, f32[4,9,16,128]{3,2,1,0:T(8,128)S(1)}, f32[4,9,16,128]{3,2,1,0:T(8,128)...) custom-call(s32[1]{0:T(128)} %bitcast.me_ref, ...), custom_call_target="tpu_custom_call" | custom-call | flops 1 | bytes 1 | tf_op jit(solution)/shard_map/pack/pallas_call | solution.py:120
  3.6 2.0 %collective-permute-start.1 = (f32[4,9,16,128]{3,2,1,0:T(8,128)S(1)}, f32[4,9,16,128]{3,2,1,0:T(8,128)S(1)}, u32[]{:S(2)}, u32[]{:S(2)}) collective-permute-start(f32[4,9,16,128]{3,2,1,0:T(8,128)S(1)} %get-tuple-element.47), channel_id=1, source_target_pairs={{0,4},{4,0},{8,12},{12,8},{16,20},{20,16},{24,28},{28,24},{1,5},{5... | collective-permute-start | bytes 884744 | tf_op jit(solution)/shard_map/ppermute | solution.py:35
  5.6 1.3 collective-permute-start.2
  6.9 2.4 %collective-permute-start.4 = (f32[4,9,16,128]{3,2,1,0:T(8,128)}, f32[4,9,16,128]{3,2,1,0:T(8,128)S(1)}, u32[]{:S(2)}, u32[]{:S(2)}) collective-permute-start(f32[4,9,16,128]{3,2,1,0:T(8,128)} %get-tuple-element.52), channel_id=1, source_target_pairs={{0,16},{4,20},{8,24},{12,28},{16,0},{20,4},{24,8},{28,12},{1,17},{... | collective-permute-start | bytes 884744 | tf_op jit(solution)/shard_map/ppermute | solution.py:35
  9.3 1.0 collective-permute-start.5
  10.3 2.0 %collective-permute-done.1.refs_3_.refs_7_.refs_11_.refs_15_.refs_6_.refs_22_.refs_14_ = f32[4,9,16,128]{3,2,1,0:T(8,128)S(1)} collective-permute-done((f32[4,9,16,128]{3,2,1,0:T(8,128)S(1)}, f32[4,9,16,128]{3,2,1,0:T(8,128)S(1)}, u32[]{:S(2)}, u32[]{:S(2)}) %collective-permute-start.1) | collective-permute-done | bytes 294944 | tf_op jit(solution)/shard_map/ppermute | solution.py:35
  12.3 3.3 %collective-permute-start.6 = (f32[4,9,16,128]{3,2,1,0:T(8,128)}, f32[4,9,16,128]{3,2,1,0:T(8,128)S(1)}, u32[]{:S(2)}, u32[]{:S(2)}) collective-permute-start(f32[4,9,16,128]{3,2,1,0:T(8,128)} %get-tuple-element.54), channel_id=1, source_target_pairs={{0,24},{4,28},{8,16},{12,20},{16,8},{20,12},{24,0},{28,4},{1,25},{... | collective-permute-start | bytes 884744 | tf_op jit(solution)/shard_map/ppermute | solution.py:35
  15.6 9.1 %collective-permute-done.2.refs_4_.refs_8_.refs_12_.refs_16_.refs_7_.refs_23_.refs_15_ = f32[4,9,16,128]{3,2,1,0:T(8,128)S(1)} collective-permute-done((f32[4,9,16,128]{3,2,1,0:T(8,128)S(1)}, f32[4,9,16,128]{3,2,1,0:T(8,128)S(1)}, u32[]{:S(2)}, u32[]{:S(2)}) %collective-permute-start.2) | collective-permute-done | bytes 294944 | tf_op jit(solution)/shard_map/ppermute | solution.py:35
  26.2 5.2 %prepare.1 = (bf16[1024,192]{1,0:T(8,128)(2,1)S(1)}, bf16[1024,192]{1,0:T(8,128)(2,1)S(1)}, bf16[1024,192]{1,0:T(8,128)(2,1)S(1)}, bf16[1024,192]{1,0:T(8,128)(2,1)S(1)}, f32[4,8,16,128]{3,2,1,0:T(8,128)S(1)}) custom-call(s32[1]{0:T(128)} %bitcast.me_ref, s32[16,4,2]{2,1,0:T(4,128)S(1)} %copy.5.pattern_ref, f32[16,4,32,64]{3,2,1,0:T(8,128)S(1)} %copy-done.1, ...), custom_call_target="tpu_custom_call" | custom-call | flops 1 | bytes 1 | tf_op jit(solution)/shard_map/prepare/pallas_call | solution.py:93
  31.5 6.9 %collective-permute-start = (f32[1,8,16,128]{3,2,1,0:T(8,128)S(1)}, f32[1,8,16,128]{3,2,1,0:T(8,128)S(1)}, u32[]{:S(2)}, u32[]{:S(2)}) collective-permute-start(f32[1,8,16,128]{3,2,1,0:T(8,128)S(1)} %slice.3), channel_id=1, source_target_pairs={{0,1},{1,2},{2,3},{4,5},{5,6},{6,7},{8,9},{9,10},{10,11},{12,13},{... | collective-permute-start | bytes 196616 | tf_op jit(solution)/shard_map/ppermute | solution.py:28
  38.4 17.5 %fluxes_0xyz0_1xyz0_2xyz0_3xy0.1 = (f32[9,64,128]{2,1,0:T(8,128)S(1)}, f32[9,64,128]{2,1,0:T(8,128)S(1)}, f32[9,64,128]{2,1,0:T(8,128)S(1)}, f32[9,64,128]{2,1,0...) custom-call(s32[1]{0:T(128)} %bitcast.me_ref, ...), custom_call_target="tpu_custom_call" | custom-call | bytes 1 | tf_op jit(solution)/shard_map/fluxes_0xyz0_1xyz0_2xyz0_3xy0/pallas_call | solution.py:289
  56.0 1.9 %collective-permute-start.8 = (f32[8,128,128]{2,1,0:T(8,128)S(1)}, f32[8,128,128]{2,1,0:T(8,128)S(1)}, u32[]{:S(2)}, u32[]{:S(2)}) collective-permute-start(f32[8,128,128]{2,1,0:T(8,128)S(1)} %get-tuple-element.56), channel_id=1, source_target_pairs={{0,1},{1,2},{2,3},{4,5},{5,6},{6,7},{8,9},{9,10},{10,11},{12,13},{... | collective-permute-start | bytes 1572872 | tf_op jit(solution)/shard_map/ppermute | solution.py:28
  58.0 2.6 %collective-permute-start.9 = (f32[8,128,128]{2,1,0:T(8,128)S(1)}, f32[8,128,128]{2,1,0:T(8,128)S(1)}, u32[]{:S(2)}, u32[]{:S(2)}) collective-permute-start(f32[8,128,128]{2,1,0:T(8,128)S(1)} %get-tuple-element.57), channel_id=1, source_target_pairs={{1,0},{2,1},{3,2},{5,4},{6,5},{7,6},{9,8},{10,9},{11,10},{13,12},{... | collective-permute-start | bytes 1572872 | tf_op jit(solution)/shard_map/ppermute | solution.py:28
  60.6 11.3 %fluxes_0xyz1_1xyz1_2xyz1_3xy1.1 = (f32[9,64,128]{2,1,0:T(8,128)S(1)}, f32[9,64,128]{2,1,0:T(8,128)S(1)}, f32[9,64,128]{2,1,0:T(8,128)S(1)}, f32[9,64,128]{2,1,0:T(8,128)S(1)}) custom-call(s32[1]{0:T(128)} %bitcast.me_ref, f32[4,8,16,128]{3,2,1,0:T(8,128)S(1)} %get-tuple-element.42.w_ref, bf16[1024,192]{1,0:T(8,128)(2,1)S(1)} %get-tuple-element.66.refs_0_.refs_1_, ...), custom_call_target="tpu_custom_call" | custom-call | flops 5905580032 | bytes 1 | tf_op jit(solution)/shard_map/fluxes_0xyz1_1xyz1_2xyz1_3xy1/pallas_call | solution.py:289
  71.9 4.0 %fluxes_3z0_-1z0_3z1_-1z1.1 = (f32[4,9,16,128]{3,2,1,0:T(8,128)S(1)}, f32[4,9,16,128]{3,2,1,0:T(8,128)S(1)}, f32[4,9,16,128]{3,2,1,0:T(8,128)S(1)}, f32[4,9,16,128]{3,2,1,0:T(8,128)S(1)}) custom-call(s32[1]{0:T(128)} %bitcast.me_ref, f32[4,8,16,128]{3,2,1,0:T(8,128)S(1)} %get-tuple-element.42.w_ref, bf16[1024,192]{1,0:T(8,128)(2,1)S(1)} %get-tuple-element.45.refs_1_.refs_0_, ...), custom_call_target="tpu_custom_call" | custom-call | flops 2147483648 | bytes 1 | tf_op jit(solution)/shard_map/fluxes_3z0_-1z0_3z1_-1z1/pallas_call | solution.py:289
  76.0 9.9 %collective-permute-start.13 = (f32[4,9,16,128]{3,2,1,0:T(8,128)S(1)}, f32[4,9,16,128]{3,2,1,0:T(8,128)S(1)}, u32[]{:S(2)}, u32[]{:S(2)}) collective-permute-start(f32[4,9,16,128]{3,2,1,0:T(8,128)S(1)} %get-tuple-element.75), channel_id=1, source_target_pairs={{0,16},{4,20},{8,24},{12,28},{16,0},{20,4},{24,8},{28,12},{1,17},{... | collective-permute-start | bytes 884744 | tf_op jit(solution)/shard_map/ppermute | solution.py:35
  86.2 3.9 %collective-permute-start.16 = (f32[4,9,16,128]{3,2,1,0:T(8,128)S(1)}, f32[4,9,16,128]{3,2,1,0:T(8,128)S(1)}, u32[]{:S(2)}, u32[]{:S(2)}) collective-permute-start(f32[4,9,16,128]{3,2,1,0:T(8,128)S(1)} %get-tuple-element.78), channel_id=1, source_target_pairs={{0,28},{4,24},{8,20},{12,16},{16,12},{20,8},{24,4},{28,0},{1,29},{... | collective-permute-start | bytes 884744 | tf_op jit(solution)/shard_map/ppermute | solution.py:35
  90.1 15.2 %fluxes_0xyz1_1xyz1_2xyz1_3xy1_3z0_-1z0_3z1_-1z1.1 = (f32[4,9,16,128]{3,2,1,0:T(8,128)S(1)}, f32[4,9,16,128]{3,2,1,0:T(8,128)S(1)}, f32[4,9,16,128]{3,2,1,0:T(8,128)S(1)}, f32[4,9,16,128]{3,2,1,0:T(8,128)S(1)}) custom-call(s32[1]{0:T(128)} %bitcast.me_ref, f32[4,8,16,128]{3,2,1,0:T(8,128)S(1)} %get-tuple-element.42.w_ref, ...), custom_call_target="tpu_custom_call" | custom-call | flops 8053063680 | bytes 1 | tf_op jit(solution)/shard_map/fluxes_0xyz1_1xyz1_2xyz1_3xy1_3z0_-1z0_3z1_-1z1/pallas_call | solution.py:289
  105.6 11.3 %collective-permute-done.13.refs_4_ = f32[4,9,16,128]{3,2,1,0:T(8,128)S(1)} collective-permute-done((f32[4,9,16,128]{3,2,1,0:T(8,128)S(1)}, f32[4,9,16,128]{3,2,1,0:T(8,128)S(1)}, u32[]{:S(2)}, u32[]{:S(2)}) %collective-permute-start.13) | collective-permute-done | bytes 294944 | tf_op jit(solution)/shard_map/ppermute | solution.py:35
  116.9 6.5 %collective-permute-done.14.refs_5_ = f32[4,9,16,128]{3,2,1,0:T(8,128)S(1)} collective-permute-done((f32[4,9,16,128]{3,2,1,0:T(8,128)S(1)}, f32[4,9,16,128]{3,2,1,0:T(8,128)S(1)}, u32[]{:S(2)}, u32[]{:S(2)}) %collective-permute-start.14) | collective-permute-done | bytes 294944 | tf_op jit(solution)/shard_map/ppermute | solution.py:35
  123.4 5.8 %collective-permute-done.11.refs_2_ = f32[4,9,16,128]{3,2,1,0:T(8,128)S(1)} collective-permute-done((f32[4,9,16,128]{3,2,1,0:T(8,128)S(1)}, f32[4,9,16,128]{3,2,1,0:T(8,128)S(1)}, u32[]{:S(2)}, u32[]{:S(2)}) %collective-permute-start.11) | collective-permute-done | bytes 294944 | tf_op jit(solution)/shard_map/ppermute | solution.py:35
  129.3 6.3 %collective-permute-done.12.refs_3_ = f32[4,9,16,128]{3,2,1,0:T(8,128)S(1)} collective-permute-done((f32[4,9,16,128]{3,2,1,0:T(8,128)S(1)}, f32[4,9,16,128]{3,2,1,0:T(8,128)S(1)}, u32[]{:S(2)}, u32[]{:S(2)}) %collective-permute-start.12) | collective-permute-done | bytes 294944 | tf_op jit(solution)/shard_map/ppermute | solution.py:35
  135.5 2.3 %unpack.1 = f32[16,4,64,128]{3,2,1,0:T(8,128)} custom-call(s32[1]{0:T(128)} %bitcast.me_ref, f32[4,9,16,128]{3,2,1,0:T(8,128)S(1)} %get-tuple-element.62.refs_0_, f32[4,9,16,128]{3,2,1,0:T(8,128)S(1)} %collective-permute-done.10.refs_1_, f32[4,9,16,128]{3,2,1,0:T(8,128)S(1)} %collective-permute-done.11.refs_2_, ...), custom_call_target="tpu_custom_call" | custom-call | flops 1 | bytes 1 | tf_op jit(solution)/shard_map/unpack/pallas_call | solution.py:335
  (28 shorter events, 2.2 us)
Async XLA Ops:
  0.0 25.1 %copy-start.3 = (s32[16,4,2]{0,2,1:T(2,128)S(1)}, s32[16,4,2]{0,2,1:T(2,128)}, u32[]{:S(2)}) copy-start(s32[16,4,2]{0,2,1:T(2,128)} %param.7) | copy-start | bytes 1540
  0.0 1.6 %copy-start = (f32[16,4,64,128]{3,2,1,0:T(8,128)S(1)}, f32[16,4,64,128]{3,2,1,0:T(8,128)}, u32[]{:S(2)}) copy-start(f32[16,4,64,128]{3,2,1,0:T(8,128)} %field_ref.3) | copy-start | bytes 6291460
  1.6 23.7 %copy-start.1 = (f32[16,4,32,64]{3,2,1,0:T(8,128)S(1)}, f32[16,4,32,64]{3,2,1,0:T(8,128)}, u32[]{:S(2)}) copy-start(f32[16,4,32,64]{3,2,1,0:T(8,128)} %blocks_ref.1) | copy-start | bytes 1572868
  3.6 8.8 %collective-permute-start.1 = (f32[4,9,16,128]{3,2,1,0:T(8,128)S(1)}, f32[4,9,16,128]{3,2,1,0:T(8,128)S(1)}, u32[]{:S(2)}, u32[]{:S(2)}) collective-permute-start(f32[4,9,16,128]{3,2,1,0:T(8,128)S(1)} %get-tuple-element.47), channel_id=1, source_target_pairs={{0,4},{4,0},{8,12},{12,8},{16,20},{20,16},{24,28},{28,24},{1,5},{5... | collective-permute-start | bytes 884744 | tf_op jit(solution)/shard_map/ppermute | solution.py:35
  5.6 19.1 %collective-permute-start.2 = (f32[4,9,16,128]{3,2,1,0:T(8,128)S(1)}, f32[4,9,16,128]{3,2,1,0:T(8,128)S(1)}, u32[]{:S(2)}, u32[]{:S(2)}) collective-permute-start(f32[4,9,16,128]{3,2,1,0:T(8,128)S(1)} %get-tuple-element.48), channel_id=1, source_target_pairs={{0,8},{4,12},{8,0},{12,4},{16,24},{20,28},{24,16},{28,20},{1,9},{5... | collective-permute-start | bytes 884744 | tf_op jit(solution)/shard_map/ppermute | solution.py:35
  6.9 24.6 %collective-permute-start.3 = (f32[4,9,16,128]{3,2,1,0:T(8,128)}, f32[4,9,16,128]{3,2,1,0:T(8,128)S(1)}, u32[]{:S(2)}, u32[]{:S(2)}) collective-permute-start(f32[4,9,16,128]{3,2,1,0:T(8,128)} %get-tuple-element.49), channel_id=1, source_target_pairs={{0,12},{4,8},{8,4},{12,0},{16,28},{20,24},{24,20},{28,16},{1,13},{... | collective-permute-start | bytes 884744 | tf_op jit(solution)/shard_map/ppermute | solution.py:35
  6.9 49.0 %collective-permute-start.4 = (f32[4,9,16,128]{3,2,1,0:T(8,128)}, f32[4,9,16,128]{3,2,1,0:T(8,128)S(1)}, u32[]{:S(2)}, u32[]{:S(2)}) collective-permute-start(f32[4,9,16,128]{3,2,1,0:T(8,128)} %get-tuple-element.52), channel_id=1, source_target_pairs={{0,16},{4,20},{8,24},{12,28},{16,0},{20,4},{24,8},{28,12},{1,17},{... | collective-permute-start | bytes 884744 | tf_op jit(solution)/shard_map/ppermute | solution.py:35
  9.3 46.6 %collective-permute-start.5 = (f32[4,9,16,128]{3,2,1,0:T(8,128)}, f32[4,9,16,128]{3,2,1,0:T(8,128)S(1)}, u32[]{:S(2)}, u32[]{:S(2)}) collective-permute-start(f32[4,9,16,128]{3,2,1,0:T(8,128)} %get-tuple-element.53), channel_id=1, source_target_pairs={{0,20},{4,16},{8,28},{12,24},{16,4},{20,0},{24,12},{28,8},{1,21},{... | collective-permute-start | bytes 884744 | tf_op jit(solution)/shard_map/ppermute | solution.py:35
  12.3 43.6 %collective-permute-start.6 = (f32[4,9,16,128]{3,2,1,0:T(8,128)}, f32[4,9,16,128]{3,2,1,0:T(8,128)S(1)}, u32[]{:S(2)}, u32[]{:S(2)}) collective-permute-start(f32[4,9,16,128]{3,2,1,0:T(8,128)} %get-tuple-element.54), channel_id=1, source_target_pairs={{0,24},{4,28},{8,16},{12,20},{16,8},{20,12},{24,0},{28,4},{1,25},{... | collective-permute-start | bytes 884744 | tf_op jit(solution)/shard_map/ppermute | solution.py:35
  24.7 31.2 %collective-permute-start.7 = (f32[4,9,16,128]{3,2,1,0:T(8,128)}, f32[4,9,16,128]{3,2,1,0:T(8,128)S(1)}, u32[]{:S(2)}, u32[]{:S(2)}) collective-permute-start(f32[4,9,16,128]{3,2,1,0:T(8,128)} %get-tuple-element.55), channel_id=1, source_target_pairs={{0,28},{4,24},{8,20},{12,16},{16,12},{20,8},{24,4},{28,0},{1,29},{... | collective-permute-start | bytes 884744 | tf_op jit(solution)/shard_map/ppermute | solution.py:35
  25.3 1.0 copy-start.2
  31.5 40.4 %collective-permute-start = (f32[1,8,16,128]{3,2,1,0:T(8,128)S(1)}, f32[1,8,16,128]{3,2,1,0:T(8,128)S(1)}, u32[]{:S(2)}, u32[]{:S(2)}) collective-permute-start(f32[1,8,16,128]{3,2,1,0:T(8,128)S(1)} %slice.3), channel_id=1, source_target_pairs={{0,1},{1,2},{2,3},{4,5},{5,6},{6,7},{8,9},{9,10},{10,11},{12,13},{... | collective-permute-start | bytes 196616 | tf_op jit(solution)/shard_map/ppermute | solution.py:28
  56.0 15.9 %collective-permute-start.8 = (f32[8,128,128]{2,1,0:T(8,128)S(1)}, f32[8,128,128]{2,1,0:T(8,128)S(1)}, u32[]{:S(2)}, u32[]{:S(2)}) collective-permute-start(f32[8,128,128]{2,1,0:T(8,128)S(1)} %get-tuple-element.56), channel_id=1, source_target_pairs={{0,1},{1,2},{2,3},{4,5},{5,6},{6,7},{8,9},{9,10},{10,11},{12,13},{... | collective-permute-start | bytes 1572872 | tf_op jit(solution)/shard_map/ppermute | solution.py:28
  58.0 13.9 %collective-permute-start.9 = (f32[8,128,128]{2,1,0:T(8,128)S(1)}, f32[8,128,128]{2,1,0:T(8,128)S(1)}, u32[]{:S(2)}, u32[]{:S(2)}) collective-permute-start(f32[8,128,128]{2,1,0:T(8,128)S(1)} %get-tuple-element.57), channel_id=1, source_target_pairs={{1,0},{2,1},{3,2},{5,4},{6,5},{7,6},{9,8},{10,9},{11,10},{13,12},{... | collective-permute-start | bytes 1572872 | tf_op jit(solution)/shard_map/ppermute | solution.py:28
  76.0 40.9 %collective-permute-start.13 = (f32[4,9,16,128]{3,2,1,0:T(8,128)S(1)}, f32[4,9,16,128]{3,2,1,0:T(8,128)S(1)}, u32[]{:S(2)}, u32[]{:S(2)}) collective-permute-start(f32[4,9,16,128]{3,2,1,0:T(8,128)S(1)} %get-tuple-element.75), channel_id=1, source_target_pairs={{0,16},{4,20},{8,24},{12,28},{16,0},{20,4},{24,8},{28,12},{1,17},{... | collective-permute-start | bytes 884744 | tf_op jit(solution)/shard_map/ppermute | solution.py:35
  85.9 37.5 %collective-permute-start.14 = (f32[4,9,16,128]{3,2,1,0:T(8,128)S(1)}, f32[4,9,16,128]{3,2,1,0:T(8,128)S(1)}, u32[]{:S(2)}, u32[]{:S(2)}) collective-permute-start(f32[4,9,16,128]{3,2,1,0:T(8,128)S(1)} %get-tuple-element.76), channel_id=1, source_target_pairs={{0,20},{4,16},{8,28},{12,24},{16,4},{20,0},{24,12},{28,8},{1,21},{... | collective-permute-start | bytes 884744 | tf_op jit(solution)/shard_map/ppermute | solution.py:35
  85.9 37.5 %collective-permute-start.15 = (f32[4,9,16,128]{3,2,1,0:T(8,128)S(1)}, f32[4,9,16,128]{3,2,1,0:T(8,128)S(1)}, u32[]{:S(2)}, u32[]{:S(2)}) collective-permute-start(f32[4,9,16,128]{3,2,1,0:T(8,128)S(1)} %get-tuple-element.77), channel_id=1, source_target_pairs={{0,24},{4,28},{8,16},{12,20},{16,8},{20,12},{24,0},{28,4},{1,25},{... | collective-permute-start | bytes 884744 | tf_op jit(solution)/shard_map/ppermute | solution.py:35
  86.2 37.2 %collective-permute-start.16 = (f32[4,9,16,128]{3,2,1,0:T(8,128)S(1)}, f32[4,9,16,128]{3,2,1,0:T(8,128)S(1)}, u32[]{:S(2)}, u32[]{:S(2)}) collective-permute-start(f32[4,9,16,128]{3,2,1,0:T(8,128)S(1)} %get-tuple-element.78), channel_id=1, source_target_pairs={{0,28},{4,24},{8,20},{12,16},{16,12},{20,8},{24,4},{28,0},{1,29},{... | collective-permute-start | bytes 884744 | tf_op jit(solution)/shard_map/ppermute | solution.py:35
  105.3 18.2 %collective-permute-start.10 = (f32[4,9,16,128]{3,2,1,0:T(8,128)S(1)}, f32[4,9,16,128]{3,2,1,0:T(8,128)S(1)}, u32[]{:S(2)}, u32[]{:S(2)}) collective-permute-start(f32[4,9,16,128]{3,2,1,0:T(8,128)S(1)} %get-tuple-element.63), channel_id=1, source_target_pairs={{0,4},{4,0},{8,12},{12,8},{16,20},{20,16},{24,28},{28,24},{1,5},{5... | collective-permute-start | bytes 884744 | tf_op jit(solution)/shard_map/ppermute | solution.py:35
  116.9 12.4 %collective-permute-start.11 = (f32[4,9,16,128]{3,2,1,0:T(8,128)S(1)}, f32[4,9,16,128]{3,2,1,0:T(8,128)S(1)}, u32[]{:S(2)}, u32[]{:S(2)}) collective-permute-start(f32[4,9,16,128]{3,2,1,0:T(8,128)S(1)} %get-tuple-element.64), channel_id=1, source_target_pairs={{0,8},{4,12},{8,0},{12,4},{16,24},{20,28},{24,16},{28,20},{1,9},{5... | collective-permute-start | bytes 884744 | tf_op jit(solution)/shard_map/ppermute | solution.py:35
  123.4 12.1 %collective-permute-start.12 = (f32[4,9,16,128]{3,2,1,0:T(8,128)S(1)}, f32[4,9,16,128]{3,2,1,0:T(8,128)S(1)}, u32[]{:S(2)}, u32[]{:S(2)}) collective-permute-start(f32[4,9,16,128]{3,2,1,0:T(8,128)S(1)} %get-tuple-element.65), channel_id=1, source_target_pairs={{0,12},{4,8},{8,4},{12,0},{16,28},{20,24},{24,20},{28,16},{1,13},{... | collective-permute-start | bytes 884744 | tf_op jit(solution)/shard_map/ppermute | solution.py:35
